TPU v7x, 32 devices: a whole 2x2x4 slice. The times are simulated.
32 devices in a mesh: dp: 8 (over y, x, core), tensor: 4 (over z).
Axes of the slice: x: 2, y: 2, z: 4, core: 2. Of those that a mesh axis runs over, the one named last changes fastest.
Arguments:
- layer_input: bfloat16 [8192, 2048], P(('dp', 'tensor')), may hold values from -6 to 6
- ln_gain: float32 [2048], replicated, may hold values from 0.5 to 1.5
- ln_bias: float32 [2048], replicated, may hold values from -1 to 1
- w_query: bfloat16 [2048, 2048], P('dp', 'tensor'), may hold values from -0.125 to 0.125
- b_query: float32 [2048], P('tensor'), may hold values from -1.5 to 1.5
- w_key: bfloat16 [2048, 2048], P('dp', 'tensor'), may hold values from -0.125 to 0.125
- b_key: float32 [2048], P('tensor'), may hold values from -1.5 to 1.5
- w_value: bfloat16 [2048, 2048], P('dp', 'tensor'), may hold values from -0.125 to 0.125
- b_value: float32 [2048], P('tensor'), may hold values from -1.5 to 1.5
- w_out: bfloat16 [2048, 2048], P('tensor', 'dp'), may hold values from -2 to 2
- b_out: float32 [2048], replicated, may hold values from -1 to 1
- w_up: bfloat16 [2048, 8192], P('dp', 'tensor'), may hold values from -0.125 to 0.125
- b_up: float32 [8192], P('tensor'), may hold values from -2.5 to 2.5
- w_down: bfloat16 [8192, 2048], P('tensor', 'dp'), may hold values from -0.125 to 0.125
- b_down: float32 [2048], replicated, may hold values from -1 to 1
- prefix: int32 [8], P('dp'), may hold values from 102 to 512
- cotangent: bfloat16 [8192, 2048], P(('dp', 'tensor')), may hold values from -6 to 6
Outputs:
- layer_out: bfloat16 [8192, 2048], P(('dp', 'tensor'))
- d_input: float32 [8192, 2048], P(('dp', 'tensor'))
- d_ln_gain: float32 [2048], replicated
- d_ln_bias: float32 [2048], replicated
- d_w_query: float32 [2048, 2048], P('dp', 'tensor')
- d_b_query: float32 [2048], P('tensor')
- d_w_key: float32 [2048, 2048], P('dp', 'tensor')
- d_b_key: float32 [2048], P('tensor')
- d_w_value: float32 [2048, 2048], P('dp', 'tensor')
- d_b_value: float32 [2048], P('tensor')
- d_w_out: float32 [2048, 2048], P('tensor', 'dp')
- d_b_out: float32 [2048], replicated
- d_w_up: float32 [2048, 8192], P('dp', 'tensor')
- d_b_up: float32 [8192], P('tensor')
- d_w_down: float32 [8192, 2048], P('tensor', 'dp')
- d_b_down: float32 [2048], replicated
All inputs are finite; a program needn't handle non-finite values.
Results may differ from a plain program's by a relative error of at most 0.012.
The roundings to bfloat16 on the way count: a program that leaves them out, or rounds other values in their place, can miss the bound.
Values may be sent and summed in bfloat16 or wider, within the bound.
A program may use at most 256 MiB of HBM per device.

v0:
```python
import math

import jax
import jax.numpy as jnp
from jax import lax
from jax.sharding import PartitionSpec as P

HEAD_DIM = 64
ROT_DIM = 32


epsilon = 1e-05
rope_base = 10000.0
masked_score = -1e30


def rotate(tensor, positions, direction):
    half_dim = ROT_DIM // 2
    freqs = rope_base ** (-(jnp.arange(half_dim).astype(jnp.float32) * 2.0 / ROT_DIM))
    angles = positions.astype(jnp.float32)[:, None] * freqs[None, :]
    cosine = jnp.cos(angles)[:, None, :]
    sine = direction * jnp.sin(angles)[:, None, :]
    first = tensor[..., :half_dim]
    second = tensor[..., half_dim:ROT_DIM]
    return jnp.concatenate(
        [first * cosine - second * sine, second * cosine + first * sine, tensor[..., ROT_DIM:]],
        axis=-1,
    )


def times_transposed(left, right):
    return lax.dot_general(
        left, right, (((1,), (1,)), ((), ())), preferred_element_type=jnp.float32
    )


def rows_transposed(left, right):
    return lax.dot_general(
        left, right, (((0,), (0,)), ((), ())), preferred_element_type=jnp.float32
    )


def on_device(
    layer_input,
    ln_gain,
    ln_bias,
    w_query,
    b_query,
    w_key,
    b_key,
    w_value,
    b_value,
    w_out,
    b_out,
    w_up,
    b_up,
    w_down,
    b_down,
    prefix,
    cotangent,
):
    local_width = w_query.shape[1]
    hidden_here = w_up.shape[1]
    heads_here = local_width // HEAD_DIM
    score_scale = 1.0 / math.sqrt(HEAD_DIM)
    prefix_len = prefix[0]
    input_float = layer_input.astype(jnp.float32)
    row_mean = jnp.mean(input_float, axis=-1, keepdims=True)
    centred = input_float - row_mean
    inverse = lax.rsqrt(jnp.mean(centred * centred, axis=-1, keepdims=True) + epsilon)
    unit_rows = centred * inverse
    normed = (unit_rows * ln_gain + ln_bias).astype(jnp.bfloat16)
    normed_all = lax.all_gather(normed, "tensor", axis=0, tiled=True)
    length = normed_all.shape[0]
    positions = jnp.arange(length)
    block_rows = min(512, length)
    block_count = length // block_rows
    pieces = (
        lax.all_gather(w_query, "dp", axis=0, tiled=True),
        lax.all_gather(w_key, "dp", axis=0, tiled=True),
        lax.all_gather(w_value, "dp", axis=0, tiled=True),
        lax.all_gather(w_up, "dp", axis=0, tiled=True),
    )
    columns = normed_all
    query_acc, key_acc, value_acc, up_acc = tuple(
        (jnp.dot(columns, piece, preferred_element_type=jnp.float32) for piece in pieces)
    )
    query_pre = (query_acc + b_query).reshape(length, heads_here, HEAD_DIM)
    key_pre = (key_acc + b_key).reshape(length, heads_here, HEAD_DIM)
    query = rotate(query_pre, positions, 1.0).astype(jnp.bfloat16)
    key = rotate(key_pre, positions, 1.0).astype(jnp.bfloat16)
    value = (value_acc + b_value).reshape(length, heads_here, HEAD_DIM).astype(jnp.bfloat16)
    up_pre = up_acc + b_up
    hidden = jax.nn.gelu(up_pre, approximate=True).astype(jnp.bfloat16)

    def scores_for(query_rows, offset):
        raw = (
            jnp.einsum("qhd,khd->hqk", query_rows, key, preferred_element_type=jnp.float32)
            * score_scale
        )
        query_pos = offset + jnp.arange(block_rows)
        seen = (positions[None, :] <= query_pos[:, None]) | (positions[None, :] < prefix_len)
        return jnp.where(seen[None], raw, masked_score)

    def attend_block(index):
        offset = index * block_rows
        query_rows = lax.dynamic_slice_in_dim(query, offset, block_rows, 0)
        scores = scores_for(query_rows, offset)
        row_max = jnp.max(scores, axis=-1, keepdims=True)
        expo = jnp.exp(scores - row_max)
        totals = jnp.sum(expo, axis=-1, keepdims=True)
        probs_low = (expo / totals).astype(jnp.bfloat16)
        out_rows = jnp.einsum("hqk,khd->qhd", probs_low, value, preferred_element_type=jnp.float32)
        return (out_rows, (row_max + jnp.log(totals))[..., 0])

    indices = jnp.arange(block_count)
    out_blocks, log_totals = lax.map(attend_block, indices)
    attn = out_blocks.reshape(length, local_width).astype(jnp.bfloat16)
    pieces = (
        lax.all_gather(w_out, "dp", axis=1, tiled=True),
        lax.all_gather(w_down, "dp", axis=1, tiled=True),
    )
    part = jnp.dot(attn, pieces[0], preferred_element_type=jnp.float32) + jnp.dot(
        hidden, pieces[1], preferred_element_type=jnp.float32
    )
    partial_value = part
    branch = lax.psum_scatter(partial_value, "tensor", scatter_dimension=0, tiled=True)
    layer_out = (input_float + branch + b_out + b_down).astype(jnp.bfloat16)
    grad_all = lax.all_gather(cotangent, "tensor", axis=0, tiled=True)
    pieces = (
        lax.all_gather(w_out, "dp", axis=1, tiled=True),
        lax.all_gather(w_down, "dp", axis=1, tiled=True),
    )
    columns = grad_all
    attn_grad = times_transposed(columns, pieces[0])
    hidden_grad = times_transposed(columns, pieces[1])
    down_joined = jnp.concatenate([attn, hidden], axis=1)
    unused, gelu_pull = jax.vjp(lambda inner: jax.nn.gelu(inner, approximate=True), up_pre)
    up_grad_low = gelu_pull(hidden_grad)[0].astype(jnp.bfloat16)
    attn_grad_low = attn_grad.astype(jnp.bfloat16).reshape(length, heads_here, HEAD_DIM)

    def back_block(carry, item):
        key_grad, value_grad = carry
        index, lse_rows = item
        offset = index * block_rows
        query_rows = lax.dynamic_slice_in_dim(query, offset, block_rows, 0)
        grad_rows = lax.dynamic_slice_in_dim(attn_grad_low, offset, block_rows, 0)
        scores = scores_for(query_rows, offset)
        probs = jnp.exp(scores - lse_rows[..., None])
        value_grad = value_grad + jnp.einsum(
            "hqk,qhd->khd",
            probs.astype(jnp.bfloat16),
            grad_rows,
            preferred_element_type=jnp.float32,
        )
        prob_grad = jnp.einsum("qhd,khd->hqk", grad_rows, value, preferred_element_type=jnp.float32)
        delta = jnp.sum(probs * prob_grad, axis=-1, keepdims=True)
        score_grad = (probs * (prob_grad - delta)).astype(jnp.bfloat16)
        query_grad = (
            jnp.einsum("hqk,khd->qhd", score_grad, key, preferred_element_type=jnp.float32)
            * score_scale
        )
        key_grad = (
            key_grad
            + jnp.einsum("hqk,qhd->khd", score_grad, query_rows, preferred_element_type=jnp.float32)
            * score_scale
        )
        return ((key_grad, value_grad), query_grad)

    state_zeros = jnp.zeros((length, heads_here, HEAD_DIM), jnp.float32)
    (key_grad, value_grad), query_blocks = lax.scan(
        back_block, (state_zeros, state_zeros), (indices, log_totals)
    )
    query_grad = query_blocks.reshape(length, heads_here, HEAD_DIM)
    q_grad_low = (
        rotate(query_grad, positions, -1.0).reshape(length, local_width).astype(jnp.bfloat16)
    )
    k_grad_low = rotate(key_grad, positions, -1.0).reshape(length, local_width).astype(jnp.bfloat16)
    v_grad_low = value_grad.reshape(length, local_width).astype(jnp.bfloat16)
    up_joined = jnp.concatenate([q_grad_low, k_grad_low, v_grad_low, up_grad_low], axis=1)
    columns = grad_all
    joined_rows = lax.psum_scatter(
        jnp.concatenate(
            [rows_transposed(columns, down_joined), rows_transposed(normed_all, up_joined)], axis=1
        ),
        "dp",
        scatter_dimension=0,
        tiled=True,
    )
    down_rows = joined_rows[:, : local_width + hidden_here]
    up_rows = joined_rows[:, local_width + hidden_here :]
    d_w_out = down_rows[:, :local_width].T
    d_w_down = down_rows[:, local_width:].T
    d_w_query = up_rows[:, :local_width]
    d_w_key = up_rows[:, local_width : 2 * local_width]
    d_w_value = up_rows[:, 2 * local_width : 3 * local_width]
    d_w_up = up_rows[:, 3 * local_width :]
    pieces = (
        lax.all_gather(w_query, "dp", axis=0, tiled=True),
        lax.all_gather(w_key, "dp", axis=0, tiled=True),
        lax.all_gather(w_value, "dp", axis=0, tiled=True),
        lax.all_gather(w_up, "dp", axis=0, tiled=True),
    )
    part = (
        times_transposed(q_grad_low, pieces[0])
        + times_transposed(k_grad_low, pieces[1])
        + times_transposed(v_grad_low, pieces[2])
        + times_transposed(up_grad_low, pieces[3])
    )
    own_grad = lax.psum_scatter(part, "tensor", scatter_dimension=0, tiled=True)
    scaled_grad = own_grad * ln_gain
    norm_part = inverse * (
        scaled_grad
        - jnp.mean(scaled_grad, axis=-1, keepdims=True)
        - unit_rows * jnp.mean(scaled_grad * unit_rows, axis=-1, keepdims=True)
    )
    cot_float = cotangent.astype(jnp.float32)
    d_input = cot_float + norm_part
    d_ln_gain, d_ln_bias, d_b_out = lax.psum(
        (
            jnp.sum(own_grad * unit_rows, axis=0),
            jnp.sum(own_grad, axis=0),
            jnp.sum(cot_float, axis=0),
        ),
        ("dp", "tensor"),
    )
    d_b_query, d_b_key, d_b_value, d_b_up = lax.psum(
        (
            jnp.sum(q_grad_low.astype(jnp.float32), axis=0),
            jnp.sum(k_grad_low.astype(jnp.float32), axis=0),
            jnp.sum(v_grad_low.astype(jnp.float32), axis=0),
            jnp.sum(up_grad_low.astype(jnp.float32), axis=0),
        ),
        "dp",
    )
    return (
        layer_out,
        d_input,
        d_ln_gain,
        d_ln_bias,
        d_w_query,
        d_b_query,
        d_w_key,
        d_b_key,
        d_w_value,
        d_b_value,
        d_w_out,
        d_b_out,
        d_w_up,
        d_b_up,
        d_w_down,
        d_b_out,
    )


def solution(mesh):
    return jax.shard_map(
        on_device,
        mesh=mesh,
        in_specs=(
            P(("dp", "tensor"), None),
            P(),
            P(),
            P("dp", "tensor"),
            P("tensor"),
            P("dp", "tensor"),
            P("tensor"),
            P("dp", "tensor"),
            P("tensor"),
            P("tensor", "dp"),
            P(),
            P("dp", "tensor"),
            P("tensor"),
            P("tensor", "dp"),
            P(),
            P("dp"),
            P(("dp", "tensor"), None),
        ),
        out_specs=(
            P(("dp", "tensor"), None),
            P(("dp", "tensor"), None),
            P(),
            P(),
            P("dp", "tensor"),
            P("tensor"),
            P("dp", "tensor"),
            P("tensor"),
            P("dp", "tensor"),
            P("tensor"),
            P("tensor", "dp"),
            P(),
            P("dp", "tensor"),
            P("tensor"),
            P("tensor", "dp"),
            P(),
        ),
        check_vma=False,
    )
```

profile of v0, /device:TPU:0, one launch (start us, length us, event | category | flops | bytes accessed | tf_op | source)
XLA Modules:
  0.0 1119.6 jit_solution(12598266879445703014)
XLA Ops:
  19.4 21.1 %all-gather.11.cloned.1.call-done = bf16[2048,512]{1,0:T(8,128)(2,1)} async-done(((bf16[256,512]{1,0:T(8,128)(2,1)}), bf16[2048,512]{1,0:T(8,128)(2,1)}) %all-gather.11.cloned.1.call-update) | async-done | bytes 2097168 | tf_op jit(solution)/shard_map/all_gather | solution.py:79
  40.5 82.9 %all-gather.9.cloned.1.call-done = bf16[1024,2048]{1,0:T(8,128)(2,1)} async-done(((bf16[256,2048]{1,0:T(8,128)(2,1)}), bf16[1024,2048]{1,0:T(8,128)(2,1)}) %all-gather.9.cloned.1.call-update) | async-done | bytes 4194320 | tf_op jit(solution)/shard_map/all_gather | solution.py:73
  128.8 23.0 %all-gather.13.cloned.1.call-done = bf16[2048,512]{1,0:T(8,128)(2,1)} async-done(((bf16[256,512]{1,0:T(8,128)(2,1)}), bf16[2048,512]{1,0:T(8,128)(2,1)}) %all-gather.13.cloned.1.call-update) | async-done | bytes 2097168 | tf_op jit(solution)/shard_map/all_gather | solution.py:80
  158.7 22.8 %all-gather.15.cloned.1.call-done = bf16[2048,512]{1,0:T(8,128)(2,1)} async-done(((bf16[256,512]{1,0:T(8,128)(2,1)}), bf16[2048,512]{1,0:T(8,128)(2,1)}) %all-gather.15.cloned.1.call-update) | async-done | bytes 2097168 | tf_op jit(solution)/shard_map/all_gather | solution.py:81
  181.5 6.2 add_convert_fusion
  187.7 35.0 %while.30 = (s32[]{:T(128)}, bf16[2,512,8,64]{1,3,2,0:T(8,128)(2,1)S(1)}, f32[2,8,512]{2,1,0:T(8,128)}, s32[2]{0:T(128)S(1)}, s32[]{:T(128)}, /*index=5*/bf16[10...) while((s32[]{:T(128)}, ...), condition=%wide.region_5.6_spmd.clone.clone, body=%wide.region_2.5_spmd.clone.clone.sunk | while | flops 1125119488 | bytes 56236232 | solution.py:117
  198.9 5.9 fusion.128
  222.7 71.0 %all-gather.23.cloned.1.call-done = bf16[1024,2048]{1,0:T(8,128)(2,1)} async-done(((bf16[256,2048]{1,0:T(8,128)(2,1)}), bf16[1024,2048]{1,0:T(8,128)(2,1)}) %all-gather.23.cloned.1.call-update) | async-done | bytes 4194320 | tf_op jit(solution)/shard_map/all_gather | solution.py:129
  293.7 6.2 convolution_convert_fusion
  299.9 135.9 %while.31 = (s32[]{:T(128)}, f32[1024,8,64]{0,2,1:T(8,128)}, f32[1024,8,64]{0,2,1:T(8,128)}, f32[2,512,8,64]{1,0,3,2:T(2,128)}, s32[2]{0:T(128)S(1)}, /*index=5*...) while((s32[]{:T(128)}, f32[1024,8,64]{0,2,1:T(8,128)}, ...), condition=%wide.region_9.10_spmd.clone.clone, body=%wide.region_7.9_spmd.clone.clone.sunk | while | flops 2726032896 | bytes 246634928 | solution.py:171
  307.8 11.5 %multiply_reduce_fusion.3 = (f32[8,512]{1,0:T(8,128)}, f32[8,512,1024]{2,1,0:T(8,128)}) fusion(f32[8,512,1024]{2,1,0:T(8,128)S(1)} %fusion.138, f32[8,512]{1,0:T(8,128)} %dynamic-slice_bitcast_fusion.2, bf16[1024,8,64]{0,2,1:T(8,128)(2,1)S(1)} %get-tuple-element.562, bf16[1024,8,64]{0,2,1:T(8,128)(2,1)} %get-tuple-element.560, s32[]{:T(128)S(6)} %select_n.46, ...), kind=kOutput, calls=%fused_computation.21.clone.1 | convolution fusion | flops 557838336 | bytes 35684356 | tf_op jit(solution)/shard_map/while/body/eval_jaxpr/qhd,khd->hqk/dot_general | solution.py:98
  319.3 10.0 multiply_convert_fusion.3
  329.3 6.7 bitcast_add_fusion.4
  347.9 19.6 %dynamic_update_slice.24 = f32[2,512,8,64]{1,0,3,2:T(2,128)} dynamic-update-slice(f32[2,512,8,64]{1,0,3,2:T(2,128)} %get-tuple-element.543, f32[1,512,8,64]{1,0,3,2:T(1,128)S(1)} %copy.64, s32[]{:T(128)S(6)} %copy.81, s32[]{:T(128)} %constant.47.clone.1..sunk.1, s32[]{:T(128)} %constant.47.clone.1..sunk.1, s32[]{:T(128)} %constant.47.clone.1..sunk.1) | dynamic-update-slice | bytes 2097156 | tf_op jit(solution)/shard_map/while/body/jit(dynamic_update_index_in_dim)/dynamic_update_slice | solution.py:117
  375.1 11.5 %multiply_reduce_fusion.3 = (f32[8,512]{1,0:T(8,128)}, f32[8,512,1024]{2,1,0:T(8,128)}) fusion(f32[8,512,1024]{2,1,0:T(8,128)S(1)} %fusion.138, f32[8,512]{1,0:T(8,128)} %dynamic-slice_bitcast_fusion.2, bf16[1024,8,64]{0,2,1:T(8,128)(2,1)S(1)} %get-tuple-element.562, bf16[1024,8,64]{0,2,1:T(8,128)(2,1)} %get-tuple-element.560, s32[]{:T(128)S(6)} %select_n.46, ...), kind=kOutput, calls=%fused_computation.21.clone.1 | convolution fusion | flops 557838336 | bytes 35684356 | tf_op jit(solution)/shard_map/while/body/eval_jaxpr/qhd,khd->hqk/dot_general | solution.py:98
  386.6 9.5 multiply_convert_fusion.3
  396.1 7.2 bitcast_add_fusion.4
  416.1 19.6 %dynamic_update_slice.24 = f32[2,512,8,64]{1,0,3,2:T(2,128)} dynamic-update-slice(f32[2,512,8,64]{1,0,3,2:T(2,128)} %get-tuple-element.543, f32[1,512,8,64]{1,0,3,2:T(1,128)S(1)} %copy.64, s32[]{:T(128)S(6)} %copy.81, s32[]{:T(128)} %constant.47.clone.1..sunk.1, s32[]{:T(128)} %constant.47.clone.1..sunk.1, s32[]{:T(128)} %constant.47.clone.1..sunk.1) | dynamic-update-slice | bytes 2097156 | tf_op jit(solution)/shard_map/while/body/jit(dynamic_update_index_in_dim)/dynamic_update_slice | solution.py:117
  457.0 14.6 %fusion.67 = f32[1024,2048]{1,0:T(8,128)} fusion(bf16[1024,2048]{1,0:T(8,128)(2,1)} %all-gather.9.cloned.1.call-done, bf16[2048,2048]{1,0:T(8,128)(2,1)} %all-gather.19.cloned.1.call-done), kind=kOutput, calls=%fused_computation.125 | convolution fusion | flops 8589934592 | bytes 20971520 | tf_op jit(solution)/shard_map/dot_general | solution.py:86
  471.6 22.0 %convert_reduce_fusion = (f32[2048]{0:T(1024)}, bf16[1024,2048]{1,0:T(8,128)(2,1)}, bf16[1024,2048]{1,0:T(8,128)(2,1)}) fusion(f32[1024,2048]{1,0:T(8,128)} %fusion.67, f32[2048]{0:T(1024)S(1)} %copy-done.33, bf16[1024,2048]{1,0:T(8,128)(2,1)} %all-gather.23.cloned.1.call-done, bf16[2048,2048]{1,0:T(8,128)(2,1)} %all-gather.21.cloned.1.call-done), kind=kOutput, calls=%fused_computation.54 | convolution fusion | flops 8642361344 | bytes 29376512 | tf_op jit(solution)/shard_map/dot_general | solution.py:32
  493.6 14.9 %fusion.71 = f32[1024,2048]{1,0:T(8,128)} fusion(bf16[1024,2048]{1,0:T(8,128)(2,1)} %get-tuple-element.327, bf16[2048,2048]{1,0:T(8,128)(2,1)} %all-gather.19.cloned.1.call-done), kind=kOutput, calls=%fused_computation.129 | convolution fusion | flops 8589934592 | bytes 20971520 | tf_op jit(solution)/shard_map/dot_general | solution.py:32
  508.6 12.0 %add_add_fusion = f32[1024,2048]{1,0:T(8,128)} fusion(f32[1024,2048]{1,0:T(8,128)} %fusion.71, f32[1024,2048]{1,0:T(8,128)S(1)} %bitcast.112, f32[1024,2048]{1,0:T(8,128)} %fusion.70, bf16[1024,512]{0,1:T(8,128)(2,1)S(1)} %bitcast.109, bf16[2048,512]{1,0:T(8,128)(2,1)S(1)} %copy-done.9), kind=kOutput, calls=%fused_computation.55 | convolution fusion | flops 2153775104 | bytes 36700160 | tf_op jit(solution)/shard_map/dot_general | solution.py:32
  523.2 11.4 %fusion.68 = f32[1024,2048]{1,0:T(8,128)S(1)} fusion(bf16[1024,2048]{1,0:T(8,128)(2,1)S(1)} %copy-done.37, bf16[2048,2048]{1,0:T(8,128)(2,1)} %all-gather.21.cloned.1.call-done), kind=kOutput, calls=%fused_computation.126 | convolution fusion | flops 8589934592 | bytes 20971520 | tf_op jit(solution)/shard_map/dot_general | solution.py:123
  534.6 6.0 convolution_add_fusion
  545.5 18.0 %convolution_bitcast_fusion = f32[2048,2560]{0,1:T(8,128)} fusion(bf16[1024,2048]{1,0:T(8,128)(2,1)} %all-gather.23.cloned.1.call-done, bf16[1024,2048]{1,0:T(8,128)(2,1)} %get-tuple-element.338, bf16[1024,512]{1,0:T(8,128)(2,1)S(1)} %copy.42), kind=kOutput, calls=%fused_computation.44 | convolution fusion | flops 10747904000 | bytes 30408704 | tf_op jit(solution)/shard_map/dot_general | solution.py:38
  563.5 20.2 %copy.46 = f32[2048,2560]{1,0:T(8,128)} copy(f32[2048,2560]{0,1:T(8,128)} %convolution_bitcast_fusion) | data formatting | bytes 41943040 | tf_op jit(solution)/shard_map/dot_general | solution.py:38
  583.7 24.0 %fusion.37 = f32[2048,3584]{1,0:T(8,128)} fusion(bf16[1024,2048]{1,0:T(8,128)(2,1)} %all-gather.9.cloned.1.call-done, bf16[1024,2048]{1,0:T(8,128)(2,1)} %get-tuple-element.327, bf16[1024,512]{1,0:T(8,128)(2,1)S(1)} %copy-done.13, bf16[1024,512]{1,0:T(8,128)(2,1)S(1)} %copy.44, bf16[1024,512]{1,0:T(8,128)(2,1)S(1)} %copy-done.14), kind=kOutput, calls=%fused_computation.57 | convolution fusion | flops 15061745664 | bytes 40894464 | tf_op jit(solution)/shard_map/dot_general | solution.py:38
  607.7 33.3 %pad_maximum_fusion = f32[2048,6144]{1,0:T(8,128)} fusion(f32[2048,3584]{1,0:T(8,128)} %fusion.37, f32[2048,2560]{1,0:T(8,128)} %copy.46), kind=kLoop, calls=%fused_computation.43 | loop fusion | flops 12582912 | bytes 100663296 | tf_op jit(solution)/shard_map/concatenate | solution.py:183
  641.9 25.6 %all-reduce.1 = (f32[512]{0:T(512)}, f32[512]{0:T(512)}, f32[512]{0:T(512)}, f32[2048]{0:T(1024)}) all-reduce(f32[512]{0:T(512)S(1)} %reduce_sum.130, f32[512]{0:T(512)S(1)} %reduce_sum.132, f32[512]{0:T(512)S(1)} %reduce_sum.134, f32[2048]{0:T(1024)S(1)} %copy-done.27), channel_id=1, replica_groups=mesh['dp'=8,'tensor'=4] {'dp'}, use_global_device_ids=true, to_apply=%region_19.20 | all-reduce | flops 3584 | bytes 28672 | tf_op jit(solution)/shard_map/psum | solution.py:227
  670.2 142.1 %reduce-scatter.4.cloned.1.call-done = f32[256,2048]{1,0:T(8,128)} async-done(((f32[1024,2048]{1,0:T(8,128)}), f32[256,2048]{1,0:T(8,128)}) %reduce-scatter.4.cloned.1.call-update) | async-done | bytes 2097168 | tf_op jit(solution)/shard_map/reduce_scatter | solution.py:127
  817.4 41.2 %all-reduce = (f32[2048]{0:T(1024)}, f32[2048]{0:T(1024)}, f32[2048]{0:T(1024)S(1)}) all-reduce(f32[2048]{0:T(1024)S(1)} %get-tuple-element.277, f32[2048]{0:T(1024)S(1)} %get-tuple-element.280, f32[2048]{0:T(1024)S(1)} %get-tuple-element.353), channel_id=1, replica_groups=mesh['dp'=8,'tensor'=4] {'dp','tensor'}, use_global_device_ids=true, to_apply=%region_14.15 | all-reduce | flops 6144 | bytes 49152 | tf_op jit(solution)/shard_map/psum | solution.py:219
  858.6 244.0 %reduce-scatter.8.cloned.1.call-done = f32[256,6144]{1,0:T(8,128)} async-done(((f32[2048,6144]{1,0:T(8,128)}), f32[256,6144]{1,0:T(8,128)}) %reduce-scatter.8.cloned.1.call-update) | async-done | bytes 6291472 | tf_op jit(solution)/shard_map/reduce_scatter | solution.py:182
  (206 shorter events, 137.3 us)
Async XLA Ops:
  7.2 33.4 %all-gather.11.cloned.1.call-start = ((), (), s32[]{:S(2)}) async-start(), calls=%async_computation.4 | async-start | bytes 2359296 | tf_op jit(solution)/shard_map/all_gather | solution.py:79
  7.9 115.6 %all-gather.9.cloned.1.call-start = ((), (), s32[]{:S(2)}) async-start(), calls=%async_computation.3 | async-start | bytes 5242880 | tf_op jit(solution)/shard_map/all_gather | solution.py:73
  9.4 114.1 %copy-start.34 = (f32[512]{0:T(512)S(1)}, f32[512]{0:T(512)}, u32[]{:S(2)}) copy-start(f32[512]{0:T(512)} %param.25) | copy-start | bytes 6148
  14.4 137.5 %all-gather.13.cloned.1.call-start = ((), (), s32[]{:S(2)}) async-start(), calls=%async_computation.5 | async-start | bytes 2359296 | tf_op jit(solution)/shard_map/all_gather | solution.py:80
  15.1 166.4 %all-gather.15.cloned.1.call-start = ((), (), s32[]{:S(2)}) async-start(), calls=%async_computation.6 | async-start | bytes 2359296 | tf_op jit(solution)/shard_map/all_gather | solution.py:81
  15.7 207.0 %all-gather.17.cloned.1.call-start = ((), (), s32[]{:S(2)}) async-start(), calls=%async_computation.7 | async-start | bytes 2359296 | tf_op jit(solution)/shard_map/all_gather | solution.py:120
  16.3 277.4 %all-gather.23.cloned.1.call-start = ((), (), s32[]{:S(2)}) async-start(), calls=%async_computation.11 | async-start | bytes 5242880 | tf_op jit(solution)/shard_map/all_gather | solution.py:129
  16.8 440.2 %all-gather.19.cloned.1.call-start = ((), (), s32[]{:S(2)}) async-start(), calls=%async_computation.8 | async-start | bytes 9437184 | tf_op jit(solution)/shard_map/all_gather | solution.py:82
  17.6 454.0 %all-gather.21.cloned.1.call-start = ((), (), s32[]{:S(2)}) async-start(), calls=%async_computation.9 | async-start | bytes 9437184 | tf_op jit(solution)/shard_map/all_gather | solution.py:121
  18.3 649.1 %reduce-scatter.6.cloned.1.call-start = ((), (), s32[]{:S(2)}) async-start(), calls=%async_computation.12 | async-start | bytes 10485760 | tf_op jit(solution)/shard_map/reduce_scatter | solution.py:210
  19.4 137.8 %copy-start.15 = (f32[1024,16]{0,1:T(8,128)}, f32[1024,16]{0,1:T(8,128)S(1)}, u32[]{:S(2)}) copy-start(f32[1024,16]{0,1:T(8,128)S(1)} %get-tuple-element.362) | copy-start | bytes 196612
  19.4 132.4 %copy-start.35 = (f32[512]{0:T(512)S(1)}, f32[512]{0:T(512)}, u32[]{:S(2)}) copy-start(f32[512]{0:T(512)} %param.27) | copy-start | bytes 6148
  157.1 24.4 %copy-start.36 = (f32[512]{0:T(512)S(1)}, f32[512]{0:T(512)}, u32[]{:S(2)}) copy-start(f32[512]{0:T(512)} %param.29) | copy-start | bytes 6148
  158.7 29.0 %copy-start.10 = (bf16[2,512,8,64]{1,3,2,0:T(8,128)(2,1)S(1)}, bf16[2,512,8,64]{1,3,2,0:T(8,128)(2,1)}, u32[]{:S(2)}) copy-start(bf16[2,512,8,64]{1,3,2,0:T(8,128)(2,1)} %custom-call.2) | copy-start | bytes 3145732
  222.7 77.2 %copy-start.11 = (bf16[2,512,8,64]{1,3,2,0:T(8,128)(2,1)}, bf16[2,512,8,64]{1,3,2,0:T(8,128)(2,1)S(1)}, u32[]{:S(2)}) copy-start(bf16[2,512,8,64]{1,3,2,0:T(8,128)(2,1)S(1)} %get-tuple-element.134) | copy-start | bytes 3145732
  346.8 20.7 %copy-start.2 = (bf16[1024,8,64]{0,2,1:T(8,128)(2,1)S(1)}, bf16[1024,8,64]{0,2,1:T(8,128)(2,1)}, u32[]{:S(2)}) copy-start(bf16[1024,8,64]{0,2,1:T(8,128)(2,1)} %copy-done.1) | copy-start | bytes 3145732 | tf_op jit(solution)/shard_map/while
  396.1 15.0 %slice-start = ((s8[8388608]{0:T(1024)(128)(4,1)}), s8[4194304]{0:T(1024)(128)(4,1)S(1)}, s32[]{:S(2)}) async-start(s8[8388608]{0:T(1024)(128)(4,1)} %bitcast.104), calls=%async_computation.14 | async-start | bytes 8388608 | tf_op jit(solution)/shard_map/while
  415.0 20.7 %copy-start.2 = (bf16[1024,8,64]{0,2,1:T(8,128)(2,1)S(1)}, bf16[1024,8,64]{0,2,1:T(8,128)(2,1)}, u32[]{:S(2)}) copy-start(bf16[1024,8,64]{0,2,1:T(8,128)(2,1)} %copy-done.1) | copy-start | bytes 3145732 | tf_op jit(solution)/shard_map/while
  493.6 15.0 %slice-start.3 = ((s8[8388608]{0:T(1024)(128)(4,1)}), s8[4194304]{0:T(1024)(128)(4,1)S(1)}, s32[]{:S(2)}) async-start(s8[8388608]{0:T(1024)(128)(4,1)} %bitcast.111), calls=%async_computation.17 | async-start | bytes 8388608
  493.6 15.0 %copy-start.9 = (bf16[2048,512]{1,0:T(8,128)(2,1)S(1)}, bf16[2048,512]{1,0:T(8,128)(2,1)}, u32[]{:S(2)}) copy-start(bf16[2048,512]{1,0:T(8,128)(2,1)} %all-gather.15.cloned.1.call-done) | copy-start | bytes 6291460
  520.7 291.7 %reduce-scatter.4.cloned.1.call-start = ((), (), s32[]{:S(2)}) async-start(), calls=%async_computation.10 | async-start | bytes 10485760 | tf_op jit(solution)/shard_map/reduce_scatter | solution.py:127
  540.6 562.0 %reduce-scatter.8.cloned.1.call-start = ((), (), s32[]{:S(2)}) async-start(), calls=%async_computation.13 | async-start | bytes 56623104 | tf_op jit(solution)/shard_map/reduce_scatter | solution.py:182
  563.5 20.2 %copy-start.13 = (bf16[1024,512]{1,0:T(8,128)(2,1)S(1)}, bf16[1024,512]{1,0:T(8,128)(2,1)}, u32[]{:S(2)}) copy-start(bf16[1024,512]{1,0:T(8,128)(2,1)} %copy.45) | copy-start | bytes 3145732
  563.5 20.2 %copy-start.14 = (bf16[1024,512]{1,0:T(8,128)(2,1)S(1)}, bf16[1024,512]{1,0:T(8,128)(2,1)}, u32[]{:S(2)}) copy-start(bf16[1024,512]{1,0:T(8,128)(2,1)} %copy.43) | copy-start | bytes 3145732
  641.0 26.4 %copy-start.5 = (bf16[256,2048]{1,0:T(8,128)(2,1)S(1)}, bf16[256,2048]{1,0:T(8,128)(2,1)}, u32[]{:S(2)}) copy-start(bf16[256,2048]{1,0:T(8,128)(2,1)} %param.21) | copy-start | bytes 3145732
  641.0 26.4 %copy-start.19 = (f32[2048]{0:T(1024)S(1)}, f32[2048]{0:T(1024)}, u32[]{:S(2)}) copy-start(f32[2048]{0:T(1024)} %param.22) | copy-start | bytes 24580
  641.0 26.4 %copy-start.21 = (f32[256]{0:T(256)S(1)}, f32[256]{0:T(256)}, u32[]{:S(2)}) copy-start(f32[256]{0:T(256)} %copy-done.20) | copy-start | bytes 3076
  641.1 26.4 %copy-start.23 = (f32[256]{0:T(256)S(1)}, f32[256]{0:T(256)}, u32[]{:S(2)}) copy-start(f32[256]{0:T(256)} %copy-done.22) | copy-start | bytes 3076
  641.1 171.3 %copy-start.29 = (f32[2048]{0:T(1024)S(1)}, f32[2048]{0:T(1024)}, u32[]{:S(2)}) copy-start(f32[2048]{0:T(1024)} %param.35) | copy-start | bytes 24580
  641.1 171.3 %copy-start.30 = (f32[2048]{0:T(1024)S(1)}, f32[2048]{0:T(1024)}, u32[]{:S(2)}) copy-start(f32[2048]{0:T(1024)} %param.31) | copy-start | bytes 24580
  667.5 144.9 %copy-start.6 = (f32[256,2048]{1,0:T(8,128)S(1)}, f32[256,2048]{1,0:T(8,128)}, u32[]{:S(2)}) copy-start(f32[256,2048]{1,0:T(8,128)} %reduce-scatter.6.cloned.1.call-done) | copy-start | bytes 6291460
  858.6 253.4 %copy-start.28 = (f32[2048]{0:T(1024)}, f32[2048]{0:T(1024)S(1)}, u32[]{:S(2)}) copy-start(f32[2048]{0:T(1024)S(1)} %get-tuple-element.601) | copy-start | bytes 24580
  (27 other events, 150.6 us)
Sparse Core Ops, SparseCore 0:
  9.9 30.5 all-gather.10
  42.7 80.7 all-gather.8
  125.4 26.4 all-gather.12
  153.6 27.8 all-gather.14
  183.2 28.1 all-gather.16
  212.9 80.7 all-gather.22
  295.6 52.9 all-gather.18
  350.5 55.8 all-gather.20
  520.8 144.0 reduce-scatter.5
  667.1 145.2 reduce-scatter.3
  816.0 286.5 reduce-scatter.7
where the time goes:
time: 1130 us; the launch traced here: 1120 us
  waiting for transfers between devices  611 us (54%)
  matrix products  239 us (21%)
  local copies, waits for them, and re-layouts  95.7 us (8%)
  other arithmetic  88.5 us (8%)
  blocking collectives  66.8 us (6%)
  between operations  14.8 us (1%)
    reduce_scatter x1, waiting for transfers between devices, on_device(): lax.psum_scatter(jnp.concatenate([rows_transposed(columns, down_joined),...  244 us
    reduce_scatter x1, waiting for transfers between devices, on_device(): lax.psum_scatter(partial_value, 'tensor', scatter_dimension=0, tiled=True)  142 us
    all_gather x1, waiting for transfers between devices, on_device(): normed_all = lax.all_gather(normed, 'tensor', axis=0, tiled=True)  82.9 us
    all_gather x1, waiting for transfers between devices, on_device(): grad_all = lax.all_gather(cotangent, 'tensor', axis=0, tiled=True)  71 us
    dot_general x6, matrix products, times_transposed(): lax.dot_general(left, right, (((1,), (1,)), ((), ())), preferred_element_...  66.5 us
    dot_general x2, matrix products, rows_transposed(): lax.dot_general(left, right, (((0,), (0,)), ((), ())), preferred_element_...  42 us
    dynamic_update_slice x4, local copies, waits for them, and re-layouts, on_device(): out_blocks, log_totals = lax.map(attend_block, indices)  41.4 us
    psum x1, blocking collectives, on_device(): lax.psum((jnp.sum(own_grad * unit_rows, axis=0), jnp.sum(own_grad, axis=0...  41.2 us
  transfers between devices with their start and end apart: 11, of which 7 were waited for; matrix products, arithmetic and copies ran while one was open for 32% of the time, Pallas kernels for 0%

commit v1 on v0

--- a/solution.py
+++ b/solution.py
@@ -1,17 +1,476 @@
+import functools
 import math
 
 import jax
 import jax.numpy as jnp
 from jax import lax
+from jax.experimental import pallas as pl
+from jax.experimental.pallas import tpu as pltpu
 from jax.sharding import PartitionSpec as P
 
 HEAD_DIM = 64
 ROT_DIM = 32
-
+MESH = pl.DeviceIdType.MESH
+BF = jnp.bfloat16
+F32 = jnp.float32
 
 epsilon = 1e-05
 rope_base = 10000.0
 masked_score = -1e30
+root = math.sqrt(2.0 / math.pi)
+
+
+def nn(a, b):
+    return jnp.dot(a, b, preferred_element_type=F32)
+
+
+def nt(a, b):
+    return lax.dot_general(a, b, (((1,), (1,)), ((), ())), preferred_element_type=F32)
+
+
+def tn(a, b):
+    return lax.dot_general(a, b, (((0,), (0,)), ((), ())), preferred_element_type=F32)
+
+
+def rows_at(index, size):
+    return pl.ds(pl.multiple_of(index * size, size), size)
+
+
+def flip(index, bit):
+    return index + bit - 2 * bit * lax.rem(index // bit, 2)
+
+
+class Copies:
+    def __init__(self, send, recv):
+        self.send, self.recv, self.count, self.sent = send, recv, 0, []
+
+    def new(self):
+        self.count += 1
+        return self.count - 1
+
+    def make(self, k, src, dst, device):
+        return pltpu.make_async_remote_copy(
+            src, dst, self.send.at[k], self.recv.at[k], device_id=device, device_id_type=MESH
+        )
+
+    def start(self, k, src, dst, device):
+        copy = self.make(k, src, dst, device)
+        copy.start()
+        self.sent.append(copy)
+
+    def wait(self, k, dst, device):
+        self.make(k, dst, dst, device).wait_recv()
+
+    def finish(self):
+        for copy in self.sent:
+            copy.wait_send()
+
+
+class Spread:
+    def __init__(self, copies, view, me, z):
+        self.c, self.view, self.me, self.z = copies, view, me, z
+        self.k = [copies.new() for _ in range(9)]
+
+    def dev(self, bit):
+        return (flip(self.me, bit), self.z)
+
+    def own(self):
+        v = self.view(self.me)
+        self.c.start(self.k[1], v, v, self.dev(2))
+        self.c.start(self.k[2], v, v, self.dev(4))
+        self.c.start(self.k[0], v, v, self.dev(1))
+
+    def forward(self):
+        c, x, y = self.c, flip(self.me, 2), flip(self.me, 4)
+        c.wait(self.k[1], self.view(x), self.dev(2))
+        v = self.view(x, 0)
+        c.start(self.k[3], v, v, self.dev(4))
+        c.wait(self.k[2], self.view(y), self.dev(4))
+        v = self.view(y, 1)
+        c.start(self.k[4], v, v, self.dev(2))
+        v = self.view(x)
+        c.start(self.k[5], v, v, self.dev(1))
+        v = self.view(y)
+        c.start(self.k[6], v, v, self.dev(1))
+
+    def last(self):
+        c, far = self.c, flip(flip(self.me, 2), 4)
+        c.wait(self.k[3], self.view(far, 0), self.dev(4))
+        c.wait(self.k[4], self.view(far, 1), self.dev(2))
+        v = self.view(far)
+        c.start(self.k[7], v, v, self.dev(1))
+
+    def ready(self):
+        c, s = self.c, flip(self.me, 1)
+        c.wait(self.k[0], self.view(s), self.dev(1))
+        c.wait(self.k[5], self.view(flip(s, 2)), self.dev(1))
+        c.wait(self.k[6], self.view(flip(s, 4)), self.dev(1))
+        c.wait(self.k[7], self.view(flip(flip(s, 2), 4)), self.dev(1))
+
+
+class Line:
+    def __init__(self, copies, buf, size, n, me, z):
+        self.c, self.buf, self.size, self.n, self.me, self.z = copies, buf, size, n, me, z
+        self.k = [(copies.new(), copies.new()) for _ in range(n - 1)]
+
+    def block(self, j):
+        return self.buf.at[rows_at(jnp.clip(j, 0, self.n - 1), self.size), :]
+
+    def start(self, s):
+        z, n = self.z, self.n
+        up, down = self.block(z - s), self.block(z + s)
+
+        @pl.when((z >= s) & (z < n - 1))
+        def _():
+            self.c.make(self.k[s][0], up, up, (self.me, jnp.minimum(z + 1, n - 1))).start()
+
+        @pl.when((z + s <= n - 1) & (z > 0))
+        def _():
+            self.c.make(self.k[s][1], down, down, (self.me, jnp.maximum(z - 1, 0))).start()
+
+    def recv(self, s):
+        z, n = self.z, self.n
+        up, down = self.block(z - 1 - s), self.block(z + 1 + s)
+
+        @pl.when(z >= s + 1)
+        def _():
+            self.c.make(self.k[s][0], up, up, (self.me, jnp.minimum(z + 1, n - 1))).wait_recv()
+
+        @pl.when(z + 1 + s <= n - 1)
+        def _():
+            self.c.make(self.k[s][1], down, down, (self.me, jnp.maximum(z - 1, 0))).wait_recv()
+
+    def finish(self):
+        z, n = self.z, self.n
+        for s in range(n - 1):
+            block = self.block(z)
+
+            @pl.when((z >= s) & (z < n - 1))
+            def _():
+                self.c.make(self.k[s][0], block, block, (self.me, jnp.minimum(z + 1, n - 1))).wait_send()
+
+            @pl.when((z + s <= n - 1) & (z > 0))
+            def _():
+                self.c.make(self.k[s][1], block, block, (self.me, jnp.maximum(z - 1, 0))).wait_send()
+
+
+def turned(x, table, sign):
+    return (
+        x * table[0]
+        + pltpu.roll(x, 112, 1) * (table[1] * sign)
+        + pltpu.roll(x, 16, 1) * (table[2] * sign)
+    )
+
+
+def gather_forward(
+    n,
+    prefix,
+    x,
+    cot,
+    wq,
+    wk,
+    wv,
+    wo,
+    wu,
+    wd,
+    gain,
+    bias,
+    bqkv,
+    bu,
+    table,
+    normed,
+    cots,
+    w_qkv,
+    w_up,
+    qkv,
+    joined,
+    branch,
+    attn_grad,
+    up_grad,
+    lse,
+    w_dn,
+    slope,
+    own_x,
+    send,
+    recv,
+    local,
+):
+    me, z = lax.axis_index("dp"), lax.axis_index("tensor")
+    size, d = x.shape
+    length = n * size
+    width = wq.shape[1]
+    ff = wu.shape[1]
+    shard = wq.shape[0]
+    lanes = wo.shape[1]
+
+    barrier = pltpu.get_barrier_semaphore()
+    for bit in (1, 2, 4):
+        pl.semaphore_signal(barrier, 1, device_id=(flip(me, bit), z), device_id_type=MESH)
+
+    @pl.when(z > 0)
+    def _():
+        pl.semaphore_signal(barrier, 1, device_id=(me, jnp.maximum(z - 1, 0)), device_id_type=MESH)
+
+    @pl.when(z < n - 1)
+    def _():
+        pl.semaphore_signal(barrier, 1, device_id=(me, jnp.minimum(z + 1, n - 1)), device_id_type=MESH)
+
+    mine, cols = rows_at(me, shard), rows_at(me, lanes)
+    loads = [
+        pltpu.make_async_copy(x, own_x, local.at[0]),
+        pltpu.make_async_copy(wq, w_qkv.at[mine, pl.ds(0, width)], local.at[1]),
+        pltpu.make_async_copy(wk, w_qkv.at[mine, pl.ds(width, width)], local.at[2]),
+        pltpu.make_async_copy(wv, w_qkv.at[mine, pl.ds(2 * width, width)], local.at[3]),
+        pltpu.make_async_copy(wu, w_up.at[mine, :], local.at[4]),
+        pltpu.make_async_copy(wo, w_dn.at[pl.ds(0, width), cols], local.at[5]),
+        pltpu.make_async_copy(wd, w_dn.at[pl.ds(width, ff), cols], local.at[6]),
+        pltpu.make_async_copy(cot, cots.at[rows_at(z, size), :], local.at[7]),
+    ]
+    for load in loads:
+        load.start()
+
+    copies = Copies(send, recv)
+
+    def row_view(buf):
+        def view(i, half=None):
+            if half is None:
+                return buf.at[rows_at(i, shard), :]
+            h = shard // 2
+            return buf.at[pl.ds(pl.multiple_of(i * shard + half * h, h), h), :]
+
+        return view
+
+    def col_view(first, count):
+        def view(i, half=None):
+            if half is None:
+                return w_dn.at[pl.ds(first, count), rows_at(i, lanes)]
+            h = count // 2
+            return w_dn.at[pl.ds(first + half * h, h), rows_at(i, lanes)]
+
+        return view
+
+    s_qkv = Spread(copies, row_view(w_qkv), me, z)
+    s_up = Spread(copies, row_view(w_up), me, z)
+    s_dn = [Spread(copies, col_view(0, width + ff // 2), me, z), Spread(copies, col_view(width + ff // 2, ff // 2), me, z)]
+    l_n = Line(copies, normed, size, n, me, z)
+    l_c = Line(copies, cots, size, n, me, z)
+
+    order = [z, flip(z, 1), flip(z, 2), flip(flip(z, 1), 2)]
+
+    def norm(r, carry):
+        rows = rows_at(r, 64)
+        v = own_x[rows, :].astype(F32)
+        mean = jnp.mean(v, axis=-1, keepdims=True)
+        c = v - mean
+        inv = lax.rsqrt(jnp.mean(c * c, axis=-1, keepdims=True) + epsilon)
+        out = (c * inv) * gain[...] + bias[...]
+        normed[pl.ds(pl.multiple_of(z * size + r * 64, 64), 64), :] = out.astype(BF)
+        return carry
+
+    def project(j):
+        rows = rows_at(j, size)
+        for part in range(3):
+            acc = nn(normed[rows, :], w_qkv[:, part * width : (part + 1) * width])
+            acc = acc + bqkv[:, part * width : (part + 1) * width]
+            for p in range(width // 128):
+                piece = acc[:, p * 128 : (p + 1) * 128]
+                if part < 2:
+                    tab = [table[i, rows, :] for i in range(3)]
+                    piece = turned(piece, tab, 1.0)
+                    if part == 0:
+                        piece = piece * (1.0 / math.sqrt(HEAD_DIM))
+                qkv[rows, part * width + p * 128 : part * width + (p + 1) * 128] = piece.astype(BF)
+
+    def raise_(j):
+        rows = rows_at(j, size)
+        tile = 512
+
+        @pl.loop(0, ff // tile)
+        def _(t):
+            cs = rows_at(t, tile)
+            u = nn(normed[rows, :], w_up[:, cs]) + bu[:, cs]
+            sq = u * u
+            th = jnp.tanh(root * u * (1.0 + 0.044715 * sq))
+            half = 0.5 * (1.0 + th)
+            joined[rows, pl.ds(pl.multiple_of(width + t * tile, tile), tile)] = (u * half).astype(BF)
+            slope[rows, cs] = (
+                half + 0.5 * u * (1.0 - th * th) * (root * (1.0 + 3 * 0.044715 * sq))
+            ).astype(BF)
+
+    def attend(first, count):
+        block = length // 4
+
+        @pl.loop(first, first + count)
+        def _(p):
+            ps = rows_at(p, 128)
+            head = lax.broadcasted_iota(jnp.int32, (1, 128), 1) // HEAD_DIM
+            for b in range(4):
+                nk = max(b + 1, 2) * block
+                qs = pl.ds(b * block, block)
+                q = qkv[qs, ps]
+                k = qkv[pl.ds(0, nk), pl.ds(pl.multiple_of(width + p * 128, 128), 128)]
+                v = qkv[pl.ds(0, nk), pl.ds(pl.multiple_of(2 * width + p * 128, 128), 128)]
+                limit = jnp.maximum(
+                    b * block + lax.broadcasted_iota(jnp.int32, (block, 1), 0), prefix[0] - 1
+                )
+                seen = lax.broadcasted_iota(jnp.int32, (block, nk), 1) <= limit
+                outs = []
+                for h in range(2):
+                    s = nt(jnp.where(head == h, q, jnp.zeros_like(q)), k)
+                    s = jnp.where(seen, s, masked_score)
+                    top = jnp.max(s, axis=-1, keepdims=True)
+                    e = jnp.exp(s - top)
+                    total = jnp.sum(e, axis=-1, keepdims=True)
+                    probs = (e * (1.0 / total)).astype(BF)
+                    outs.append(nn(probs, v))
+                    lane = lax.broadcasted_iota(jnp.int32, (1, 128), 1)
+                    lse[qs, :] = jnp.where(lane == 2 * p + h, top + jnp.log(total), lse[qs, :])
+                joined[qs, ps] = jnp.where(head == 0, outs[0], outs[1]).astype(BF)
+
+    def lower(j):
+        rows = rows_at(j, size)
+        tile = 512
+
+        @pl.loop(0, d // tile)
+        def _(t):
+            branch[rows, rows_at(t, tile)] = nn(joined[rows, :], w_dn[:, rows_at(t, tile)]).astype(BF)
+
+    def back_down(j):
+        rows = rows_at(j, size)
+        tile = 512
+        attn_grad[rows, :] = nt(cots[rows, :], w_dn[:width, :]).astype(BF)
+
+        @pl.loop(0, ff // tile)
+        def _(t):
+            g = nt(cots[rows, :], w_dn[pl.ds(pl.multiple_of(width + t * tile, tile), tile), :])
+            cs = rows_at(t, tile)
+            up_grad[rows, cs] = (g * slope[rows, cs].astype(F32)).astype(BF)
+
+    signals = 3 + jnp.where(z > 0, 1, 0) + jnp.where(z < n - 1, 1, 0)
+    pl.semaphore_wait(barrier, signals)
+
+    for i in (1, 2, 3):
+        loads[i].wait()
+    s_qkv.own()
+    loads[0].wait()
+    lax.fori_loop(0, size // 64, norm, 0)
+    l_n.start(0)
+    loads[4].wait()
+    s_up.own()
+    lse[...] = jnp.zeros_like(lse)
+    s_qkv.forward()
+    l_n.recv(0)
+    l_n.start(1)
+    s_qkv.last()
+    loads[5].wait()
+    loads[6].wait()
+    s_dn[0].own()
+    s_qkv.ready()
+    project(order[0])
+    s_up.forward()
+    project(order[1])
+    l_n.recv(1)
+    l_n.start(2)
+    s_up.last()
+    s_dn[1].own()
+    project(order[2])
+    s_up.ready()
+    raise_(order[0])
+    s_dn[0].forward()
+    raise_(order[1])
+    l_n.recv(2)
+    loads[7].wait()
+    l_c.start(0)
+    s_dn[0].last()
+    project(order[3])
+    raise_(order[2])
+    s_dn[1].forward()
+    raise_(order[3])
+    attend(0, 2)
+    l_c.recv(0)
+    l_c.start(1)
+    s_dn[1].last()
+    attend(2, 2)
+    for s in s_dn:
+        s.ready()
+    back_down(order[0])
+    back_down(order[1])
+    l_c.recv(1)
+    l_c.start(2)
+    lower(order[0])
+    lower(order[1])
+    lower(order[2])
+    lower(order[3])
+    back_down(order[2])
+    l_c.recv(2)
+    back_down(order[3])
+    l_n.finish()
+    l_c.finish()
+    copies.finish()
+
+
+def tables(length):
+    half = ROT_DIM // 2
+    freqs = rope_base ** (-(jnp.arange(half).astype(F32) * 2.0 / ROT_DIM))
+    angles = jnp.arange(length).astype(F32)[:, None] * freqs[None, :]
+    cos, sin = jnp.cos(angles), jnp.sin(angles)
+    one, zero = jnp.ones((length, HEAD_DIM - ROT_DIM), F32), jnp.zeros((length, half), F32)
+    wide = jnp.zeros((length, HEAD_DIM - ROT_DIM), F32)
+    c = jnp.concatenate([cos, cos, one], 1)
+    s1 = jnp.concatenate([-sin, zero, wide], 1)
+    s2 = jnp.concatenate([zero, sin, wide], 1)
+    return jnp.stack([jnp.concatenate([t, t], 1) for t in (c, s1, s2)])
+
+
+def forward_call(n, prefix, x, cot, wq, wk, wv, wo, wu, wd, gain, bias, bq, bk, bv, bu):
+    size, d = x.shape
+    length, width, ff = n * size, wq.shape[1], wu.shape[1]
+    vm, hbm = pl.BlockSpec(memory_space=pltpu.VMEM), pl.BlockSpec(memory_space=pl.ANY)
+    shape = lambda s, t=BF: jax.ShapeDtypeStruct(s, t)
+    return pl.pallas_call(
+        functools.partial(gather_forward, n),
+        out_shape=(
+            shape((length, d)),
+            shape((length, d)),
+            shape((d, 3 * width)),
+            shape((d, ff)),
+            shape((length, 3 * width)),
+            shape((length, width + ff)),
+            shape((length, d)),
+            shape((length, width)),
+            shape((length, ff)),
+            shape((length, 128), F32),
+        ),
+        in_specs=[pl.BlockSpec(memory_space=pltpu.SMEM)] + [hbm] * 8 + [vm] * 5,
+        out_specs=(vm,) * 10,
+        scratch_shapes=[
+            pltpu.VMEM((width + ff, d), BF),
+            pltpu.VMEM((length, ff), BF),
+            pltpu.VMEM((size, d), BF),
+            pltpu.SemaphoreType.DMA((48,)),
+            pltpu.SemaphoreType.DMA((48,)),
+            pltpu.SemaphoreType.DMA((8,)),
+        ],
+        compiler_params=pltpu.CompilerParams(
+            collective_id=1, has_side_effects=True, vmem_limit_bytes=63 << 20
+        ),
+        cost_estimate=pl.CostEstimate(flops=50_000_000_000, bytes_accessed=100_000_000, transcendentals=0),
+    )(
+        prefix,
+        x,
+        cot,
+        wq,
+        wk,
+        wv,
+        wo,
+        wu,
+        wd,
+        gain[None],
+        bias[None],
+        jnp.concatenate([bq, bk, bv])[None],
+        bu[None],
+        tables(length),
+    )
 
 
 def rotate(tensor, positions, direction):
@@ -40,7 +499,7 @@
     )
 
 
-def on_device(
+def plain_on_device(
     layer_input,
     ln_gain,
     ln_bias,
@@ -253,9 +712,124 @@
     )
 
 
+def on_device(
+    layer_input, ln_gain, ln_bias, w_query, b_query, w_key, b_key, w_value, b_value,
+    w_out, b_out, w_up, b_up, w_down, b_down, prefix, cotangent,
+):
+    n = lax.axis_size("tensor")
+    local_width = w_query.shape[1]
+    hidden_here = w_up.shape[1]
+    heads_here = local_width // HEAD_DIM
+    score_scale = 1.0 / math.sqrt(HEAD_DIM)
+    prefix_len = prefix[0]
+    input_float = layer_input.astype(jnp.float32)
+    row_mean = jnp.mean(input_float, axis=-1, keepdims=True)
+    centred = input_float - row_mean
+    inverse = lax.rsqrt(jnp.mean(centred * centred, axis=-1, keepdims=True) + epsilon)
+    unit_rows = centred * inverse
+    normed_all, grad_all, w_qkv, w_up_all, qkv, joined, part, attn_grad, up_grad_low, lse = forward_call(
+        n, prefix, layer_input, cotangent, w_query, w_key, w_value, w_out, w_up, w_down,
+        ln_gain, ln_bias, b_query, b_key, b_value, b_up,
+    )
+    length = normed_all.shape[0]
+    positions = jnp.arange(length)
+    block_rows = min(512, length)
+    block_count = length // block_rows
+    query, key, value = (
+        qkv[:, i * local_width : (i + 1) * local_width].reshape(length, heads_here, HEAD_DIM)
+        for i in range(3)
+    )
+    log_totals = lse[:, :heads_here].T.reshape(heads_here, block_count, block_rows).transpose(1, 0, 2)
+
+    def scores_for(query_rows, offset):
+        raw = jnp.einsum("qhd,khd->hqk", query_rows, key, preferred_element_type=jnp.float32)
+        query_pos = offset + jnp.arange(block_rows)
+        seen = (positions[None, :] <= query_pos[:, None]) | (positions[None, :] < prefix_len)
+        return jnp.where(seen[None], raw, masked_score)
+
+    indices = jnp.arange(block_count)
+    branch = lax.psum_scatter(part.astype(F32), "tensor", scatter_dimension=0, tiled=True)
+    layer_out = (input_float + branch + b_out + b_down).astype(jnp.bfloat16)
+    attn_grad_low = attn_grad.reshape(length, heads_here, HEAD_DIM)
+
+    def back_block(carry, item):
+        key_grad, value_grad = carry
+        index, lse_rows = item
+        offset = index * block_rows
+        query_rows = lax.dynamic_slice_in_dim(query, offset, block_rows, 0)
+        grad_rows = lax.dynamic_slice_in_dim(attn_grad_low, offset, block_rows, 0)
+        scores = scores_for(query_rows, offset)
+        probs = jnp.exp(scores - lse_rows[..., None])
+        value_grad = value_grad + jnp.einsum(
+            "hqk,qhd->khd", probs.astype(jnp.bfloat16), grad_rows, preferred_element_type=jnp.float32
+        )
+        prob_grad = jnp.einsum("qhd,khd->hqk", grad_rows, value, preferred_element_type=jnp.float32)
+        delta = jnp.sum(probs * prob_grad, axis=-1, keepdims=True)
+        score_grad = (probs * (prob_grad - delta)).astype(jnp.bfloat16)
+        query_grad = (
+            jnp.einsum("hqk,khd->qhd", score_grad, key, preferred_element_type=jnp.float32) * score_scale
+        )
+        key_grad = key_grad + jnp.einsum(
+            "hqk,qhd->khd", score_grad, query_rows, preferred_element_type=jnp.float32
+        )
+        return ((key_grad, value_grad), query_grad)
+
+    state_zeros = jnp.zeros((length, heads_here, HEAD_DIM), jnp.float32)
+    (key_grad, value_grad), query_blocks = lax.scan(
+        back_block, (state_zeros, state_zeros), (indices, log_totals)
+    )
+    query_grad = query_blocks.reshape(length, heads_here, HEAD_DIM)
+    q_grad_low = rotate(query_grad, positions, -1.0).reshape(length, local_width).astype(jnp.bfloat16)
+    k_grad_low = rotate(key_grad, positions, -1.0).reshape(length, local_width).astype(jnp.bfloat16)
+    v_grad_low = value_grad.reshape(length, local_width).astype(jnp.bfloat16)
+    up_joined = jnp.concatenate([q_grad_low, k_grad_low, v_grad_low, up_grad_low], axis=1)
+    joined_rows = lax.psum_scatter(
+        jnp.concatenate(
+            [rows_transposed(grad_all, joined), rows_transposed(normed_all, up_joined)], axis=1
+        ),
+        "dp",
+        scatter_dimension=0,
+        tiled=True,
+    )
+    down_rows = joined_rows[:, : local_width + hidden_here]
+    up_rows = joined_rows[:, local_width + hidden_here :]
+    d_w_out = down_rows[:, :local_width].T
+    d_w_down = down_rows[:, local_width:].T
+    d_w_query = up_rows[:, :local_width]
+    d_w_key = up_rows[:, local_width : 2 * local_width]
+    d_w_value = up_rows[:, 2 * local_width : 3 * local_width]
+    d_w_up = up_rows[:, 3 * local_width :]
+    part = times_transposed(up_joined[:, : 3 * local_width], w_qkv) + times_transposed(up_grad_low, w_up_all)
+    own_grad = lax.psum_scatter(part, "tensor", scatter_dimension=0, tiled=True)
+    scaled_grad = own_grad * ln_gain
+    norm_part = inverse * (
+        scaled_grad
+        - jnp.mean(scaled_grad, axis=-1, keepdims=True)
+        - unit_rows * jnp.mean(scaled_grad * unit_rows, axis=-1, keepdims=True)
+    )
+    cot_float = cotangent.astype(jnp.float32)
+    d_input = cot_float + norm_part
+    d_ln_gain, d_ln_bias, d_b_out = lax.psum(
+        (
+            jnp.sum(own_grad * unit_rows, axis=0),
+            jnp.sum(own_grad, axis=0),
+            jnp.sum(cot_float, axis=0),
+        ),
+        ("dp", "tensor"),
+    )
+    sums = lax.psum(jnp.sum(up_joined.astype(jnp.float32), axis=0), "dp")
+    d_b_query, d_b_key, d_b_value = (sums[i * local_width : (i + 1) * local_width] for i in range(3))
+    d_b_up = sums[3 * local_width :]
+    return (
+        layer_out, d_input, d_ln_gain, d_ln_bias, d_w_query, d_b_query, d_w_key, d_b_key,
+        d_w_value, d_b_value, d_w_out, d_b_out, d_w_up, d_b_up, d_w_down, d_b_out,
+    )
+
+
 def solution(mesh):
+    fits = mesh.shape["dp"] == 8 and mesh.shape["tensor"] == 4
     return jax.shard_map(
-        on_device,
+        on_device if fits else plain_on_device,
         mesh=mesh,
         in_specs=(
             P(("dp", "tensor"), None),

time: 1130 us -> 983 us (0.87)
  waiting for transfers between devices: 611 us -> 415 us
  Pallas kernels: 0 us -> 187 us
  matrix products: 239 us -> 125 us
  local copies, waits for them, and re-layouts: 95.7 us -> 83.9 us
    all_gather x8 -> x0, waiting for transfers between devices: 221 us -> none  [the longest x1 82.9 us: on_device(): normed_all = lax.all_gather(normed, 'tensor', axis=0, tiled=True)]
    pallas_call x0 -> x1, Pallas kernels: none -> 187 us  [forward_call(): pl.pallas_call(functools.partial(gather_forward, n), out_shape=(shape((le...]
    dot_general x8 -> x0, matrix products: 60.4 us -> none  [the longest x4 31.3 us: on_device(): jnp.dot(columns, piece, preferred_element_type=jnp.float32)]
    dot_general x6 -> x2, matrix products: 66.5 us -> 22.1 us  [times_transposed(): lax.dot_general(left, right, (((1,), (1,)), ((), ())), preferred_element_...]
    reduce_scatter x1, waiting for transfers between devices: 0.01 us -> 26.1 us  [on_device(): own_grad = lax.psum_scatter(part, 'tensor', scatter_dimension=0, tiled=True)]
    dot_general x4 -> x2, matrix products: 31.3 us -> 7.25 us  [scores_for(): jnp.einsum('qhd,khd->hqk', query_rows, key, preferred_element_type=jnp.fl...]
    dot_general x1 -> x0, local copies, waits for them, and re-layouts: 20.2 us -> none  [rows_transposed(): lax.dot_general(left, right, (((0,), (0,)), ((), ())), preferred_element_...]
    dot_general x2, matrix products: 7.69 us -> 22.5 us  [back_block(): jnp.einsum('qhd,khd->hqk', grad_rows, value, preferred_element_type=jnp.f...]
  transfers between devices with their start and end apart: 11 -> 3, of which waited for: 7 -> 3; matrix products, arithmetic and copies ran while one was open for 32% -> 10% of each run, Pallas kernels for 0% -> 0%
where the time goes in v1:
time: 983 us; the launch traced here: 976 us
  waiting for transfers between devices  415 us (42%)
  Pallas kernels  187 us (19%)
  matrix products  125 us (13%)
  local copies, waits for them, and re-layouts  83.9 us (9%)
  other arithmetic  83 us (8%)
  blocking collectives  65.3 us (7%)
  between operations  15 us (2%)
    reduce_scatter x1, waiting for transfers between devices, on_device(): lax.psum_scatter(jnp.concatenate([rows_transposed(grad_all, joined), rows...  244 us
    pallas_call x1, Pallas kernels, forward_call(): pl.pallas_call(functools.partial(gather_forward, n), out_shape=(shape((le...  187 us
    reduce_scatter x1, waiting for transfers between devices, on_device(): lax.psum_scatter(part.astype(F32), 'tensor', scatter_dimension=0, tiled=T...  145 us
    dynamic_update_slice x4, local copies, waits for them, and re-layouts, on_device(): lax.scan(back_block, (state_zeros, state_zeros), (indices, log_totals))  43.6 us
    dot_general x2, matrix products, rows_transposed(): lax.dot_general(left, right, (((0,), (0,)), ((), ())), preferred_element_...  42.2 us
    psum x1, blocking collectives, on_device(): lax.psum((jnp.sum(own_grad * unit_rows, axis=0), jnp.sum(own_grad, axis=0...  41.2 us
    concatenate x1, other arithmetic, on_device(): jnp.concatenate([rows_transposed(grad_all, joined), rows_transposed(norme...  34.1 us
    reduce_scatter x1, waiting for transfers between devices, on_device(): own_grad = lax.psum_scatter(part, 'tensor', scatter_dimension=0, tiled=True)  26.1 us
  transfers between devices with their start and end apart: 3, of which 3 were waited for; matrix products, arithmetic and copies ran while one was open for 10% of the time, Pallas kernels for 0%

profile of v1, /device:TPU:0, one launch (start us, length us, event | category | flops | bytes accessed | tf_op | source)
XLA Modules:
  0.0 975.8 jit_solution(9467238114404278960)
XLA Ops:
  17.6 186.6 %shard_map.288 = (bf16[1024,2048]{1,0:T(8,128)(2,1)}, bf16[1024,2048]{1,0:T(8,128)(2,1)}, bf16[2048,1536]{1,0:T(8,128)(2,1)}, bf16[2048,2048]{1,0:T(8,128)(2,1)}...) custom-call(s32[1]{0:T(128)S(6)} %copy.98.prefix, ...), custom_call_target="tpu_custom_call" | custom-call | flops 49999998976 | bytes 100000000 | tf_op jit(solution)/shard_map/pallas_call | solution.py:430
  213.6 132.0 %while.16 = (s32[]{:T(128)}, f32[1024,8,64]{0,2,1:T(8,128)}, f32[1024,8,64]{0,2,1:T(8,128)}, f32[2,512,8,64]{1,0,3,2:T(2,128)}, s32[2]{0:T(128)S(1)}, /*index=5*...) while((s32[]{:T(128)}, f32[1024,8,64]{0,2,1:T(8,128)}, ...), condition=%wide.region_5.6_spmd.clone.clone, body=%wide.region_3.5_spmd.clone.clone.sunk | while | flops 2738091520 | bytes 203610544 | solution.py:778
  216.8 3.6 fusion.82
  220.5 5.6 bitcast_add_fusion.5
  226.1 11.2 %multiply_reduce_fusion.3 = (f32[8,512]{1,0:T(8,128)}, f32[8,512,1024]{2,1,0:T(8,128)}) fusion(f32[8,512,1024]{2,1,0:T(8,128)S(1)} %fusion.82, f32[8,512]{1,0:T(8,128)} %copy-done.8, pred[512,1024]{1,0:T(8,128)(4,1)} %copy-done.1, bf16[1024,8,64]{0,2,1:T(8,128)(2,1)} %get-tuple-element.400, bf16[1024,8,64]{0,2,1:T(8,128)(2,1)} %get-tuple-element.399, ...), kind=kOutput, calls=%fused_computation.2.clone.1 | convolution fusion | flops 553644032 | bytes 35684356 | tf_op jit(solution)/shard_map/while/body/eval_jaxpr/qhd,khd->hqk/dot_general | solution.py:766
  237.3 10.5 %multiply_convert_fusion.2 = bf16[8,512,1024]{2,1,0:T(8,128)(2,1)} fusion(f32[8,512,1024]{2,1,0:T(8,128)} %get-tuple-element.358, f32[8,512,1024]{2,1,0:T(8,128)S(1)} %fusion.82, f32[8,512]{1,0:T(8,128)} %get-tuple-element.359, f32[8,512]{1,0:T(8,128)} %copy-done.8, pred[512,1024]{1,0:T(8,128)(4,1)} %copy-done.1), kind=kLoop, calls=%fused_computation.1.clone.1 | loop fusion | flops 20971520 | bytes 42500096 | tf_op jit(solution)/shard_map/while/body/eval_jaxpr/convert_element_type | solution.py:768
  247.8 6.2 fusion.84
  254.2 2.9 bitcast_add_fusion.4
  259.2 19.6 %dynamic_update_slice.7 = f32[2,512,8,64]{1,0,3,2:T(2,128)} dynamic-update-slice(f32[2,512,8,64]{1,0,3,2:T(2,128)} %get-tuple-element.378, f32[1,512,8,64]{1,0,3,2:T(1,128)} %copy.83, s32[]{:T(128)S(6)} %copy.89, s32[]{:T(128)} %constant.46.clone.1..sunk, s32[]{:T(128)} %constant.46.clone.1..sunk, s32[]{:T(128)} %constant.46.clone.1..sunk) | dynamic-update-slice | bytes 2097156 | tf_op jit(solution)/shard_map/while/body/jit(dynamic_update_index_in_dim)/dynamic_update_slice | solution.py:778
  281.9 3.6 fusion.82
  285.6 6.8 bitcast_add_fusion.5
  292.4 11.2 %multiply_reduce_fusion.3 = (f32[8,512]{1,0:T(8,128)}, f32[8,512,1024]{2,1,0:T(8,128)}) fusion(f32[8,512,1024]{2,1,0:T(8,128)S(1)} %fusion.82, f32[8,512]{1,0:T(8,128)} %copy-done.8, pred[512,1024]{1,0:T(8,128)(4,1)} %copy-done.1, bf16[1024,8,64]{0,2,1:T(8,128)(2,1)} %get-tuple-element.400, bf16[1024,8,64]{0,2,1:T(8,128)(2,1)} %get-tuple-element.399, ...), kind=kOutput, calls=%fused_computation.2.clone.1 | convolution fusion | flops 553644032 | bytes 35684356 | tf_op jit(solution)/shard_map/while/body/eval_jaxpr/qhd,khd->hqk/dot_general | solution.py:766
  303.6 10.5 %multiply_convert_fusion.2 = bf16[8,512,1024]{2,1,0:T(8,128)(2,1)} fusion(f32[8,512,1024]{2,1,0:T(8,128)} %get-tuple-element.358, f32[8,512,1024]{2,1,0:T(8,128)S(1)} %fusion.82, f32[8,512]{1,0:T(8,128)} %get-tuple-element.359, f32[8,512]{1,0:T(8,128)} %copy-done.8, pred[512,1024]{1,0:T(8,128)(4,1)} %copy-done.1), kind=kLoop, calls=%fused_computation.1.clone.1 | loop fusion | flops 20971520 | bytes 42500096 | tf_op jit(solution)/shard_map/while/body/eval_jaxpr/convert_element_type | solution.py:768
  314.1 6.2 fusion.84
  320.5 2.9 bitcast_add_fusion.4
  325.5 19.6 %dynamic_update_slice.7 = f32[2,512,8,64]{1,0,3,2:T(2,128)} dynamic-update-slice(f32[2,512,8,64]{1,0,3,2:T(2,128)} %get-tuple-element.378, f32[1,512,8,64]{1,0,3,2:T(1,128)} %copy.83, s32[]{:T(128)S(6)} %copy.89, s32[]{:T(128)} %constant.46.clone.1..sunk, s32[]{:T(128)} %constant.46.clone.1..sunk, s32[]{:T(128)} %constant.46.clone.1..sunk) | dynamic-update-slice | bytes 2097156 | tf_op jit(solution)/shard_map/while/body/jit(dynamic_update_index_in_dim)/dynamic_update_slice | solution.py:778
  345.6 4.2 reshape.200
  354.0 11.3 %fusion.48 = f32[1024,2048]{1,0:T(8,128)S(1)} fusion(bf16[1024,2048]{1,0:T(8,128)(2,1)S(1)} %copy-done.10, bf16[2048,2048]{1,0:T(8,128)(2,1)} %get-tuple-element.102), kind=kOutput, calls=%fused_computation.84 | convolution fusion | flops 8589934592 | bytes 20971520 | tf_op jit(solution)/shard_map/dot_general | solution.py:491
  366.5 10.9 %convolution_add_fusion = f32[1024,2048]{1,0:T(8,128)} fusion(f32[1024,2048]{1,0:T(8,128)S(1)} %fusion.48, bf16[2048,1536]{1,0:T(8,128)(2,1)} %get-tuple-element.100, bf16[1024,512]{0,1:T(8,128)(2,1)S(1)} %bitcast.71, bf16[1024,512]{0,1:T(8,128)(2,1)S(1)} %bitcast.75, bf16[1024,512]{0,1:T(8,128)(2,1)S(1)} %bitcast.73), kind=kOutput, calls=%fused_computation.32 | convolution fusion | flops 6453985280 | bytes 26214400 | tf_op jit(solution)/shard_map/dot_general | solution.py:491
  377.4 6.8 convert_element_type.116
  387.7 18.5 %fusion.49 = f32[2048,2560]{1,0:T(8,128)} fusion(bf16[1024,2048]{1,0:T(8,128)(2,1)} %get-tuple-element.103, bf16[1024,2560]{1,0:T(8,128)(2,1)} %get-tuple-element.104), kind=kOutput, calls=%fused_computation.85 | convolution fusion | flops 10737418240 | bytes 30408704 | tf_op jit(solution)/shard_map/dot_general | solution.py:497
  406.2 23.8 %fusion.41 = f32[2048,3584]{1,0:T(8,128)} fusion(bf16[1024,2048]{1,0:T(8,128)(2,1)} %get-tuple-element.105, bf16[1024,2048]{1,0:T(8,128)(2,1)} %get-tuple-element.101, bf16[1024,512]{1,0:T(8,128)(2,1)S(1)} %copy-done.13, bf16[1024,512]{1,0:T(8,128)(2,1)S(1)} %copy.68, bf16[1024,512]{1,0:T(8,128)(2,1)S(1)} %copy.67), kind=kOutput, calls=%fused_computation.59 | convolution fusion | flops 15061745664 | bytes 40894464 | tf_op jit(solution)/shard_map/dot_general | solution.py:497
  430.0 34.1 %pad_maximum_fusion = f32[2048,6144]{1,0:T(8,128)} fusion(f32[2048,3584]{1,0:T(8,128)} %fusion.41, f32[2048,2560]{1,0:T(8,128)} %fusion.49), kind=kLoop, calls=%fused_computation.29 | loop fusion | flops 12582912 | bytes 100663296 | tf_op jit(solution)/shard_map/concatenate | solution.py:787
  465.3 3.7 convert_reduce_fusion
  469.1 24.1 %psum.30 = f32[3584]{0:T(1024)S(1)} all-reduce(f32[3584]{0:T(1024)S(1)} %convert_reduce_fusion), channel_id=1, replica_groups=mesh['dp'=8,'tensor'=4] {'dp'}, use_global_device_ids=true, to_apply=%region_15.16 | all-reduce | flops 3584 | bytes 28672 | tf_op jit(solution)/shard_map/psum | solution.py:820
  495.1 26.1 %reduce-scatter.6.cloned.1.call-done = f32[256,2048]{1,0:T(8,128)} async-done(((f32[1024,2048]{1,0:T(8,128)}), f32[256,2048]{1,0:T(8,128)}) %reduce-scatter.6.cloned.1.call-update) | async-done | bytes 2097168 | tf_op jit(solution)/shard_map/reduce_scatter | solution.py:803
  521.2 2.7 fusion.36
  523.9 144.9 %reduce-scatter.4.cloned.1.call-done = f32[256,2048]{1,0:T(8,128)} async-done(((f32[1024,2048]{1,0:T(8,128)}), f32[256,2048]{1,0:T(8,128)}) %reduce-scatter.4.cloned.1.call-update) | async-done | bytes 2097168 | tf_op jit(solution)/shard_map/reduce_scatter | solution.py:751
  668.8 5.0 convert_reduce_fusion.2
  673.8 41.2 %all-reduce = (f32[2048]{0:T(1024)}, f32[2048]{0:T(1024)}, f32[2048]{0:T(1024)S(1)}) all-reduce(f32[2048]{0:T(1024)S(1)} %get-tuple-element.231, f32[2048]{0:T(1024)S(1)} %get-tuple-element.234, f32[2048]{0:T(1024)S(1)} %get-tuple-element.275), channel_id=1, replica_groups=mesh['dp'=8,'tensor'=4] {'dp','tensor'}, use_global_device_ids=true, to_apply=%region_10.11 | all-reduce | flops 6144 | bytes 49152 | tf_op jit(solution)/shard_map/psum | solution.py:812
  715.0 244.0 %reduce-scatter.8.cloned.1.call-done = f32[256,6144]{1,0:T(8,128)} async-done(((f32[2048,6144]{1,0:T(8,128)}), f32[256,6144]{1,0:T(8,128)}) %reduce-scatter.8.cloned.1.call-update) | async-done | bytes 6291472 | tf_op jit(solution)/shard_map/reduce_scatter | solution.py:786
  959.0 3.9 slice_bitcast_fusion
  (116 shorter events, 46.3 us)
Async XLA Ops:
  7.2 514.0 %reduce-scatter.6.cloned.1.call-start = ((), (), s32[]{:S(2)}) async-start(), calls=%async_computation.4 | async-start | bytes 10485760 | tf_op jit(solution)/shard_map/reduce_scatter | solution.py:803
  216.4 4.1 copy-start.8
  216.8 3.7 copy-start.1
  216.8 3.7 copy-start.5
  247.8 6.2 copy-start
  247.8 6.4 copy-start.2
  257.1 21.8 %copy-start.3 = (f32[1024,8,64]{0,2,1:T(8,128)}, f32[1024,8,64]{0,2,1:T(8,128)S(1)}, u32[]{:S(2)}) copy-start(f32[1024,8,64]{0,2,1:T(8,128)S(1)} %bitcast_add_fusion.4) | copy-start | bytes 6291460 | tf_op jit(solution)/shard_map/while
  281.5 4.1 copy-start.8
  281.9 3.7 copy-start.1
  281.9 3.7 copy-start.5
  314.1 6.2 copy-start
  314.1 6.4 copy-start.2
  323.4 21.8 %copy-start.3 = (f32[1024,8,64]{0,2,1:T(8,128)}, f32[1024,8,64]{0,2,1:T(8,128)S(1)}, u32[]{:S(2)}) copy-start(f32[1024,8,64]{0,2,1:T(8,128)S(1)} %bitcast_add_fusion.4) | copy-start | bytes 6291460 | tf_op jit(solution)/shard_map/while
  345.6 5.6 copy-start.4
  345.6 8.1 copy-start.15
  345.6 8.1 copy-start.16
  349.8 3.9 copy-start.9
  349.8 4.3 copy-start.10
  365.5 1.0 copy-start.14
  377.4 291.4 %reduce-scatter.4.cloned.1.call-start = ((), (), s32[]{:S(2)}) async-start(), calls=%async_computation.3 | async-start | bytes 10485760 | tf_op jit(solution)/shard_map/reduce_scatter | solution.py:751
  384.3 574.7 %reduce-scatter.8.cloned.1.call-start = ((), (), s32[]{:S(2)}) async-start(), calls=%async_computation.5 | async-start | bytes 56623104 | tf_op jit(solution)/shard_map/reduce_scatter | solution.py:786
  386.4 19.8 %copy-start.11 = (bf16[1024,512]{1,0:T(8,128)(2,1)}, bf16[1024,512]{1,0:T(8,128)(2,1)S(1)}, u32[]{:S(2)}) copy-start(bf16[1024,512]{1,0:T(8,128)(2,1)S(1)} %copy.67) | copy-start | bytes 3145732
  387.7 18.5 %copy-start.13 = (bf16[1024,512]{1,0:T(8,128)(2,1)S(1)}, bf16[1024,512]{1,0:T(8,128)(2,1)}, u32[]{:S(2)}) copy-start(bf16[1024,512]{1,0:T(8,128)(2,1)} %copy.69) | copy-start | bytes 3145732
  464.1 1.3 copy-start.12
  465.3 28.5 %copy-start.6 = (bf16[256,2048]{1,0:T(8,128)(2,1)S(1)}, bf16[256,2048]{1,0:T(8,128)(2,1)}, u32[]{:S(2)}) copy-start(bf16[256,2048]{1,0:T(8,128)(2,1)} %x.1) | copy-start | bytes 3145732
  465.3 55.8 %copy-start.17 = (f32[2048]{0:T(1024)S(1)}, f32[2048]{0:T(1024)}, u32[]{:S(2)}) copy-start(f32[2048]{0:T(1024)} %param.20) | copy-start | bytes 24580
  469.1 199.7 %copy-start.19 = (f32[2048]{0:T(1024)S(1)}, f32[2048]{0:T(1024)}, u32[]{:S(2)}) copy-start(f32[2048]{0:T(1024)} %param.33) | copy-start | bytes 24580
  469.1 199.7 %copy-start.20 = (f32[2048]{0:T(1024)S(1)}, f32[2048]{0:T(1024)}, u32[]{:S(2)}) copy-start(f32[2048]{0:T(1024)} %param.29) | copy-start | bytes 24580
  521.2 147.6 %copy-start.7 = (f32[256,2048]{1,0:T(8,128)S(1)}, f32[256,2048]{1,0:T(8,128)}, u32[]{:S(2)}) copy-start(f32[256,2048]{1,0:T(8,128)} %reduce-scatter.6.cloned.1.call-done) | copy-start | bytes 6291460
  715.0 253.4 %copy-start.18 = (f32[2048]{0:T(1024)}, f32[2048]{0:T(1024)S(1)}, u32[]{:S(2)}) copy-start(f32[2048]{0:T(1024)S(1)} %get-tuple-element.436) | copy-start | bytes 24580
Sparse Core Ops, SparseCore 0:
  377.5 143.6 reduce-scatter.5
  523.5 145.1 reduce-scatter.3
  672.4 286.5 reduce-scatter.7

commit v2 on v1

--- a/solution.py
+++ b/solution.py
@@ -3,6 +3,7 @@
 
 import jax
 import jax.numpy as jnp
+import numpy as np
 from jax import lax
 from jax.experimental import pallas as pl
 from jax.experimental.pallas import tpu as pltpu
@@ -187,10 +188,11 @@
     branch,
     attn_grad,
     up_grad,
-    lse,
+    lse_out,
     w_dn,
     slope,
     own_x,
+    lse,
     send,
     recv,
     local,
@@ -391,6 +393,7 @@
     l_c.start(1)
     s_dn[1].last()
     attend(2, 2)
+    lse_out[...] = lse[...].T[: lse_out.shape[0], :]
     for s in s_dn:
         s.ready()
     back_down(order[0])
@@ -411,15 +414,15 @@
 
 def tables(length):
     half = ROT_DIM // 2
-    freqs = rope_base ** (-(jnp.arange(half).astype(F32) * 2.0 / ROT_DIM))
-    angles = jnp.arange(length).astype(F32)[:, None] * freqs[None, :]
-    cos, sin = jnp.cos(angles), jnp.sin(angles)
-    one, zero = jnp.ones((length, HEAD_DIM - ROT_DIM), F32), jnp.zeros((length, half), F32)
-    wide = jnp.zeros((length, HEAD_DIM - ROT_DIM), F32)
-    c = jnp.concatenate([cos, cos, one], 1)
-    s1 = jnp.concatenate([-sin, zero, wide], 1)
-    s2 = jnp.concatenate([zero, sin, wide], 1)
-    return jnp.stack([jnp.concatenate([t, t], 1) for t in (c, s1, s2)])
+    freqs = rope_base ** (-(np.arange(half).astype(np.float32) * 2.0 / ROT_DIM))
+    angles = np.arange(length).astype(np.float32)[:, None] * freqs[None, :].astype(np.float32)
+    cos, sin = np.cos(angles), np.sin(angles)
+    rest = np.zeros((length, HEAD_DIM - ROT_DIM), np.float32)
+    none = np.zeros((length, half), np.float32)
+    c = np.concatenate([cos, cos, rest + 1.0], 1)
+    s1 = np.concatenate([-sin, none, rest], 1)
+    s2 = np.concatenate([none, sin, rest], 1)
+    return jnp.asarray(np.stack([np.concatenate([t, t], 1) for t in (c, s1, s2)]).astype(np.float32))
 
 
 def forward_call(n, prefix, x, cot, wq, wk, wv, wo, wu, wd, gain, bias, bq, bk, bv, bu):
@@ -439,7 +442,7 @@
             shape((length, d)),
             shape((length, width)),
             shape((length, ff)),
-            shape((length, 128), F32),
+            shape((width // HEAD_DIM, length), F32),
         ),
         in_specs=[pl.BlockSpec(memory_space=pltpu.SMEM)] + [hbm] * 8 + [vm] * 5,
         out_specs=(vm,) * 10,
@@ -447,6 +450,7 @@
             pltpu.VMEM((width + ff, d), BF),
             pltpu.VMEM((length, ff), BF),
             pltpu.VMEM((size, d), BF),
+            pltpu.VMEM((length, 128), F32),
             pltpu.SemaphoreType.DMA((48,)),
             pltpu.SemaphoreType.DMA((48,)),
             pltpu.SemaphoreType.DMA((8,)),
@@ -470,6 +474,637 @@
         jnp.concatenate([bq, bk, bv])[None],
         bu[None],
         tables(length),
+    )
+
+
+class Fold:
+    def __init__(self, part, slots, send, recv, first, size, n, me, z):
+        self.part, self.slots, self.send, self.recv, self.first = part, slots, send, recv, first
+        self.size, self.n, self.me, self.z = size, n, me, z
+
+    def copy(self, way, s, block):
+        z, n = self.z, self.n
+        to = jnp.minimum(z + 1, n - 1) if way == 0 else jnp.maximum(z - 1, 0)
+        return pltpu.make_async_remote_copy(
+            self.part.at[rows_at(block, self.size), :],
+            self.slots.at[way, s],
+            self.send.at[self.first + way * (n - 1) + s],
+            self.recv.at[self.first + way * (n - 1) + s],
+            device_id=(self.me, to),
+            device_id_type=MESH,
+        )
+
+    def step(self, tau):
+        n = self.n
+        for way in range(2):
+            far = self.z if way == 0 else n - 1 - self.z
+            s = jnp.clip(tau - far, 0, n - 2)
+            goal = n - 1 - s if way == 0 else s
+            if tau > 0:
+
+                @pl.when((far >= 1) & (far <= tau))
+                def _():
+                    self.copy(way, s, goal).wait_recv()
+
+            if 0 < tau < n - 1:
+
+                @pl.when((far >= 1) & (far <= tau))
+                def _():
+                    @pl.loop(0, self.size // 64)
+                    def _(r):
+                        rows = pl.ds(pl.multiple_of(goal * self.size + r * 64, 64), 64)
+                        self.part[rows, :] = (
+                            self.part[rows, :].astype(F32) + self.slots[way, s, rows_at(r, 64), :].astype(F32)
+                        ).astype(BF)
+
+            if tau < n - 1:
+
+                @pl.when(far <= tau)
+                def _():
+                    self.copy(way, s, goal).start()
+
+    def own(self, r, count):
+        z, n = self.z, self.n
+        up = self.slots[0, jnp.clip(n - 1 - z, 0, n - 2), rows_at(r, count), :].astype(F32)
+        down = self.slots[1, jnp.clip(z, 0, n - 2), rows_at(r, count), :].astype(F32)
+        here = self.part[pl.ds(pl.multiple_of(z * self.size + r * count, count), count), :].astype(F32)
+        up = jnp.where(z > 0, up, jnp.zeros_like(up))
+        down = jnp.where(z < n - 1, down, jnp.zeros_like(down))
+        return here + up + down
+
+    def finish(self):
+        n = self.n
+        for s in range(n - 1):
+            for way in range(2):
+                far = self.z if way == 0 else n - 1 - self.z
+
+                @pl.when(n - 1 - s - far > 0)
+                def _():
+                    self.copy(way, s, self.z).wait_send()
+
+
+PIECE = 512
+OWN_SLOTS = 4
+SIB_SLOTS = 4
+LAG = 2
+LINK_SLOTS = 2 + 2 * LAG
+
+
+def backward_scatter(
+    n,
+    prefix,
+    x,
+    normed,
+    cots,
+    w_qkv,
+    w_up,
+    qkv,
+    joined,
+    branch,
+    attn_grad,
+    up_grad,
+    lse,
+    table,
+    gain,
+    b_sum,
+    layer_out,
+    d_input,
+    d_in,
+    d_dn,
+    d_bias,
+    d_all,
+    own_x,
+    cot,
+    grads,
+    d_attn,
+    n_block,
+    n_turned,
+    j_block,
+    j_turned,
+    wq_block,
+    wu_block,
+    part_b,
+    part_g,
+    fold_slots,
+    sib_out,
+    sib_in,
+    own_low,
+    own_sum,
+    link_in,
+    acc,
+    d_rows,
+    narrow,
+    wide,
+    wide_z,
+    sums,
+    fold_send,
+    fold_recv,
+    sib_send,
+    sib_recv,
+    link_send,
+    link_recv,
+    out_sem,
+    local,
+    stream,
+    small_send,
+    small_recv,
+    zfree,
+):
+    me, z = lax.axis_index("dp"), lax.axis_index("tensor")
+    size, d = x.shape
+    length = n * size
+    width = attn_grad.shape[1]
+    ff = up_grad.shape[1]
+    lanes = d // 8
+    down_pieces = (width + ff) // PIECE
+    up_pieces = (3 * width + ff) // PIECE
+    pieces = down_pieces + up_pieces
+    core = lax.rem(me, 2)
+    sib = (flip(me, 1), z)
+
+    barrier = pltpu.get_barrier_semaphore()
+    peers = []
+    for k in range(1, 8):
+        to = me
+        for bit in (1, 2, 4):
+            if k & bit:
+                to = flip(to, bit)
+        peers.append(to)
+        pl.semaphore_signal(barrier, 1, device_id=(to, z), device_id_type=MESH)
+    others = [lax.rem(z + k, n) for k in range(1, n)]
+    for to in others:
+        pl.semaphore_signal(barrier, 1, device_id=(me, to), device_id_type=MESH)
+
+    def load(k, src, dst):
+        return pltpu.make_async_copy(src, dst, local.at[k])
+
+    loads = [
+        load(0, branch, part_b),
+        load(1, cots, cot),
+        load(2, qkv, grads.at[:, pl.ds(0, 3 * width)]),
+        load(3, attn_grad, d_attn),
+        load(4, up_grad, grads.at[:, pl.ds(3 * width, ff)]),
+        load(5, x, own_x),
+    ]
+
+    def j_load(p):
+        return pltpu.make_async_copy(
+            joined.at[:, rows_at(jnp.minimum(p, down_pieces - 1), PIECE)],
+            j_block.at[lax.rem(p, 2)],
+            stream.at[lax.rem(p, 2)],
+        )
+
+    def w_loads(t):
+        return [
+            pltpu.make_async_copy(w_qkv.at[rows_at(t, PIECE), :], wq_block, stream.at[2]),
+            pltpu.make_async_copy(w_up.at[rows_at(t, PIECE), :], wu_block, stream.at[3]),
+        ]
+
+    def n_load(j):
+        return pltpu.make_async_copy(normed.at[rows_at(j, size), :], n_block, stream.at[4])
+
+    j_load(0).start()
+    for l in loads:
+        l.start()
+    for l in w_loads(0) + [n_load(0)]:
+        l.start()
+
+    fold_b = Fold(part_b, fold_slots, fold_send, fold_recv, 0, size, n, me, z)
+    fold_g = Fold(part_g, fold_slots, fold_send, fold_recv, 2 * (n - 1), size, n, me, z)
+
+    links = [flip(flip(me, 2), 4), flip(me, 2), flip(me, 4)]
+    goals = links + [me]
+
+    def sib_copy(p):
+        return pltpu.make_async_remote_copy(
+            sib_out.at[lax.rem(p, 2)],
+            sib_in.at[lax.rem(p, SIB_SLOTS)],
+            sib_send.at[lax.rem(p, 2)],
+            sib_recv.at[lax.rem(p, SIB_SLOTS)],
+            device_id=sib,
+            device_id_type=MESH,
+        )
+
+    def link_copy(p, r):
+        return pltpu.make_async_remote_copy(
+            own_low.at[lax.rem(p, OWN_SLOTS), r],
+            link_in.at[lax.rem(p, LINK_SLOTS), r],
+            link_send.at[lax.rem(p, OWN_SLOTS), r],
+            link_recv.at[lax.rem(p, LINK_SLOTS), r],
+            device_id=(links[r], z),
+            device_id_type=MESH,
+        )
+
+    def out_copies(p):
+        src = own_sum.at[lax.rem(p, OWN_SLOTS)]
+        sem = out_sem.at[lax.rem(p, OWN_SLOTS)]
+        half = PIECE // 2
+        down = [
+            pltpu.make_async_copy(
+                src.at[:, pl.ds(i * half, half)],
+                d_dn.at[pl.ds(pl.multiple_of(jnp.minimum(p, down_pieces - 1) * PIECE + i * half, half), half), :],
+                sem.at[i],
+            )
+            for i in range(2)
+        ]
+        up = [
+            pltpu.make_async_copy(
+                src.at[:, pl.ds(i * half, half)],
+                d_in.at[
+                    :,
+                    pl.ds(
+                        pl.multiple_of(up_column(p) + i * half, half),
+                        half,
+                    ),
+                ],
+                sem.at[i],
+            )
+            for i in range(2)
+        ]
+        return down, up
+
+    def up_column(p):
+        t = jnp.clip(p - down_pieces, 0, up_pieces - 1)
+        return lax.rem(t + 3 * width // PIECE, up_pieces) * PIECE
+
+    def first_down(p):
+        slot, out = lax.rem(p, OWN_SLOTS), lax.rem(p, 2)
+        j_load(p).wait()
+
+        @pl.when(p + 1 < down_pieces)
+        def _():
+            j_load(p + 1).start()
+
+        j_turned[...] = j_block[lax.rem(p, 2)].T
+        half = PIECE // 2
+        for r, goal in enumerate(goals):
+            for mine in range(2):
+                to = flip(goal, 1) if mine == 0 else goal
+                t = nn(j_turned[...], cot[:, rows_at(to, lanes)])
+                for i in range(2):
+                    v = t[i * half : (i + 1) * half, :]
+                    cs = pl.ds(i * half, half)
+                    if mine == 0:
+                        sib_out[out, r, :, cs] = v.astype(BF)
+                    elif r < 3:
+                        own_low[slot, r, :, cs] = v.astype(BF)
+                    else:
+                        own_sum[slot, :, cs] = v
+
+    def first_up(p):
+        slot, out = lax.rem(p, OWN_SLOTS), lax.rem(p, 2)
+        g = grads[:, pl.ds(pl.multiple_of(up_column(p), PIECE), PIECE)]
+        for r, goal in enumerate(goals):
+            for mine in range(2):
+                to = flip(goal, 1) if mine == 0 else goal
+                t = nn(n_turned[rows_at(to, lanes), :], g)
+                if mine == 0:
+                    sib_out[out, r] = t.astype(BF)
+                elif r < 3:
+                    own_low[slot, r] = t.astype(BF)
+                else:
+                    own_sum[slot] = t
+
+    def stage_one(p):
+        @pl.when(p >= 2)
+        def _():
+            sib_copy(p - 2).wait_send()
+
+        @pl.when(p >= OWN_SLOTS)
+        def _():
+            for c in out_copies(p - OWN_SLOTS)[0]:
+                c.wait()
+
+        @pl.when(p < down_pieces)
+        def _():
+            first_down(p)
+
+        @pl.when(p >= down_pieces)
+        def _():
+            first_up(p)
+
+        sib_copy(p).start()
+
+    def stage_two(p):
+        slot = lax.rem(p, OWN_SLOTS)
+        inn = lax.rem(p, SIB_SLOTS)
+        sib_copy(p).wait_recv()
+        for r in range(3):
+            own_low[slot, r] = (own_low[slot, r].astype(F32) + sib_in[inn, r].astype(F32)).astype(BF)
+            link_copy(p, r).start()
+        own_sum[slot] = own_sum[slot] + sib_in[inn, 3].astype(F32)
+
+    def stage_three(p):
+        slot = lax.rem(p, OWN_SLOTS)
+        inn = lax.rem(p, LINK_SLOTS)
+        for r in range(3):
+            link_copy(p, r).wait_recv()
+        own_sum[slot] = (
+            (own_sum[slot] + link_in[inn, 0].astype(F32)) + link_in[inn, 1].astype(F32)
+        ) + link_in[inn, 2].astype(F32)
+        for r in range(3):
+            link_copy(p, r).wait_send()
+        down, up = out_copies(p)
+
+        @pl.when(p < down_pieces)
+        def _():
+            for c in down:
+                c.start()
+
+        @pl.when(p >= down_pieces)
+        def _():
+            for c in up:
+                c.start()
+
+    def attend_back(p):
+        block = length // 4
+        ps = rows_at(p, 128)
+        ks = pl.ds(pl.multiple_of(width + p * 128, 128), 128)
+        vs = pl.ds(pl.multiple_of(2 * width + p * 128, 128), 128)
+        head = lax.broadcasted_iota(jnp.int32, (1, 128), 1) // HEAD_DIM
+        acc[...] = jnp.zeros_like(acc)
+        for b in range(4):
+            nk = max(b + 1, 2) * block
+            qs, kr = pl.ds(b * block, block), pl.ds(0, nk)
+            limit = jnp.maximum(
+                b * block + lax.broadcasted_iota(jnp.int32, (1, block), 1), prefix[0] - 1
+            )
+
+            @pl.loop(0, 2)
+            def _(h):
+                only = lambda a: jnp.where(head == h, a, jnp.zeros_like(a))
+                k, v = grads[kr, ks], grads[kr, vs]
+                qh, gh = only(grads[qs, ps]), only(d_attn[qs, ps])
+                s = nt(k, qh)
+                seen = lax.broadcasted_iota(jnp.int32, (nk, block), 0) <= limit
+                probs = jnp.where(seen, jnp.exp(s - lse[pl.ds(2 * p + h, 1), qs]), 0.0)
+                acc[2, kr, :] += nn(probs.astype(BF), gh)
+                dp = nt(v, gh)
+                delta = jnp.sum(probs * dp, axis=0, keepdims=True)
+                ds = (probs * (dp - delta)).astype(BF)
+                acc[1, kr, :] += nn(ds, qh)
+                acc[0, qs, :] += tn(ds, only(k)) * (1.0 / math.sqrt(HEAD_DIM))
+
+        tab = [table[i] for i in range(3)]
+        grads[:, ps] = turned(acc[0], tab, -1.0).astype(BF)
+        grads[:, ks] = turned(acc[1], tab, -1.0).astype(BF)
+        grads[:, vs] = acc[2].astype(BF)
+
+    def normed_back(t):
+        for l in w_loads(t):
+            l.wait()
+
+        @pl.loop(0, length // 512)
+        def _(m):
+            rows = rows_at(m, 512)
+            part_g[rows, t * PIECE : (t + 1) * PIECE] = (
+                nt(grads[rows, : 3 * width], wq_block[...]) + nt(grads[rows, 3 * width :], wu_block[...])
+            ).astype(BF)
+
+        if t + 1 < d // PIECE:
+            for l in w_loads(t + 1):
+                l.start()
+
+    def turn(j):
+        n_load(j).wait()
+        n_turned[:, j * size : (j + 1) * size] = n_block[...].T
+        if j + 1 < n:
+            n_load(j + 1).start()
+
+    def small(k, src, dst, to):
+        return pltpu.make_async_remote_copy(
+            src, dst, small_send.at[k], small_recv.at[k], device_id=to, device_id_type=MESH
+        )
+
+    def bias_sums():
+        for i in range(up_pieces):
+            narrow[me, i : i + 1, :] = jnp.sum(
+                grads[:, i * PIECE : (i + 1) * PIECE].astype(F32), axis=0, keepdims=True
+            )
+        for k, to in enumerate(peers):
+            small(k, narrow.at[me], narrow.at[me], (to, z)).start()
+
+    def branch_end():
+        loads[5].wait()
+
+        @pl.loop(0, size // 32)
+        def _(r):
+            rows = pl.ds(pl.multiple_of(z * size + r * 32, 32), 32)
+            v = own_x[rows_at(r, 32), :].astype(F32) + fold_b.own(r, 32) + b_sum[0:1, :] + b_sum[1:2, :]
+            part_b[rows, :] = v.astype(BF)
+
+        out = load(0, part_b.at[rows_at(z, size), :], layer_out)
+        out.start()
+        fold_b.finish()
+
+        @pl.when(z > 0)
+        def _():
+            pl.semaphore_signal(zfree.at[0], 1, device_id=(me, jnp.maximum(z - 1, 0)), device_id_type=MESH)
+
+        @pl.when(z < n - 1)
+        def _():
+            pl.semaphore_signal(zfree.at[1], 1, device_id=(me, jnp.minimum(z + 1, n - 1)), device_id_type=MESH)
+
+        out.wait()
+
+    def fold_free():
+        @pl.when(z < n - 1)
+        def _():
+            pl.semaphore_wait(zfree.at[0], 1)
+
+        @pl.when(z > 0)
+        def _():
+            pl.semaphore_wait(zfree.at[1], 1)
+
+    def input_end():
+        sums[...] = jnp.zeros_like(sums)
+
+        def chunk(r):
+            return pltpu.make_async_copy(
+                d_rows.at[lax.rem(r, 2)], d_input.at[rows_at(r, 32), :], local.at[lax.rem(r, 2)]
+            )
+
+        @pl.loop(0, size // 32)
+        def _(r):
+            grad = fold_g.own(r, 32)
+            v = own_x[rows_at(r, 32), :].astype(F32)
+            c = v - jnp.mean(v, axis=-1, keepdims=True)
+            inv = lax.rsqrt(jnp.mean(c * c, axis=-1, keepdims=True) + epsilon)
+            unit = c * inv
+            own_cot = cot[pl.ds(pl.multiple_of(z * size + r * 32, 32), 32), :].astype(F32)
+            gu = grad * unit
+            sums[0:1, :] += jnp.sum(gu, axis=0, keepdims=True)
+            sums[1:2, :] += jnp.sum(grad, axis=0, keepdims=True)
+            sums[2:3, :] += jnp.sum(own_cot, axis=0, keepdims=True)
+            scaled = grad * gain[...]
+
+            @pl.when(r >= 2)
+            def _():
+                chunk(r - 2).wait()
+
+            d_rows[lax.rem(r, 2)] = own_cot + inv * (
+                scaled
+                - jnp.mean(scaled, axis=-1, keepdims=True)
+                - unit * jnp.mean(scaled * unit, axis=-1, keepdims=True)
+            )
+            chunk(r).start()
+
+        for i in range(3):
+            for q in range(4):
+                wide[me, 4 * i + q : 4 * i + q + 1, :] = sums[i : i + 1, q * PIECE : (q + 1) * PIECE]
+        for k, to in enumerate(peers):
+            small(8 + k, wide.at[me], wide.at[me], (to, z)).start()
+        for k, to in enumerate(peers):
+            small(8 + k, wide.at[to], wide.at[to], (to, z)).wait_recv()
+        total = wide[0]
+        for i in range(1, 8):
+            total = total + wide[i]
+        wide_z[z] = total
+        for k, to in enumerate(others):
+            small(16 + k, wide_z.at[z], wide_z.at[z], (me, to)).start()
+        for k in range(n - 1):
+            origin = lax.rem(z + n - 1 - k, n)
+            small(16 + k, wide_z.at[origin], wide_z.at[origin], (me, origin)).wait_recv()
+        total = wide_z[0]
+        for i in range(1, n):
+            total = total + wide_z[i]
+        d_all[...] = total
+        for k, to in enumerate(peers):
+            small(k, narrow.at[to], narrow.at[to], (to, z)).wait_recv()
+        total = narrow[0]
+        for i in range(1, 8):
+            total = total + narrow[i]
+        d_bias[...] = total
+        for k, to in enumerate(peers):
+            small(k, narrow.at[me], narrow.at[me], (to, z)).wait_send()
+            small(8 + k, wide.at[me], wide.at[me], (to, z)).wait_send()
+        for k, to in enumerate(others):
+            small(16 + k, wide_z.at[z], wide_z.at[z], (me, to)).wait_send()
+        for r in range(2):
+            chunk(size // 32 - 2 + r).wait()
+
+    narrow[me] = jnp.zeros(narrow.shape[1:], F32)
+    wide[me] = jnp.zeros(wide.shape[1:], F32)
+    pl.semaphore_wait(barrier, 7 + n - 1)
+
+    tasks = {}
+
+    def at(p, *work):
+        tasks.setdefault(p, []).extend(work)
+
+    loads[0].wait()
+    fold_b.step(0)
+    for l in loads[1:5]:
+        l.wait()
+
+    at(2, lambda: fold_b.step(1))
+    at(4, lambda: turn(0), lambda: normed_back(0), lambda: turn(1), bias_sums, lambda: turn(2), lambda: fold_b.step(2))
+    at(4, lambda: turn(3))
+    at(5, lambda: normed_back(1))
+    at(6, lambda: normed_back(2))
+    at(7, lambda: normed_back(3), lambda: fold_b.step(3), branch_end, fold_free, lambda: fold_g.step(0))
+    at(9, lambda: fold_g.step(1))
+    at(11, lambda: fold_g.step(2))
+    at(13, lambda: fold_g.step(3))
+
+    @pl.loop(0, pieces + 1 + LAG)
+    def _(p):
+        @pl.when(p < pieces)
+        def _():
+            stage_one(p)
+
+        @pl.when((p >= 1) & (p <= pieces))
+        def _():
+            stage_two(p - 1)
+
+        @pl.when(p >= 1 + LAG)
+        def _():
+            stage_three(p - 1 - LAG)
+
+        @pl.when(p < width // 128)
+        def _():
+            attend_back(p)
+
+        for k, work in tasks.items():
+
+            @pl.when(p == k)
+            def _():
+                for w in work:
+                    w()
+
+    for p in range(2):
+        sib_copy(pieces - 2 + p).wait_send()
+    for p in range(OWN_SLOTS):
+        for c in out_copies(pieces - OWN_SLOTS + p)[1]:
+            c.wait()
+    input_end()
+    fold_g.finish()
+
+
+def backward_call(n, prefix, x, normed, cots, w_qkv, w_up, qkv, joined, branch, attn_grad, up_grad, lse, gain, b_out, b_down):
+    size, d = x.shape
+    length, width, ff = n * size, attn_grad.shape[1], up_grad.shape[1]
+    vm, hbm = pl.BlockSpec(memory_space=pltpu.VMEM), pl.BlockSpec(memory_space=pl.ANY)
+    shape = lambda s, t=BF: jax.ShapeDtypeStruct(s, t)
+    dma = pltpu.SemaphoreType.DMA
+    half = PIECE // 2
+    return pl.pallas_call(
+        functools.partial(backward_scatter, n),
+        out_shape=(
+            shape((size, d)),
+            shape((size, d), F32),
+            shape((d // 8, 3 * width + ff), F32),
+            shape((width + ff, d // 8), F32),
+            shape((8, PIECE), F32),
+            shape((16, PIECE), F32),
+        ),
+        in_specs=[pl.BlockSpec(memory_space=pltpu.SMEM)] + [hbm] * 10 + [vm] * 4,
+        out_specs=(hbm,) * 4 + (vm,) * 2,
+        scratch_shapes=[
+            pltpu.VMEM((size, d), BF),
+            pltpu.VMEM((length, d), BF),
+            pltpu.VMEM((length, 3 * width + ff), BF),
+            pltpu.VMEM((length, width), BF),
+            pltpu.VMEM((size, d), BF),
+            pltpu.VMEM((d, length), BF),
+            pltpu.VMEM((2, length, PIECE), BF),
+            pltpu.VMEM((PIECE, length), BF),
+            pltpu.VMEM((PIECE, 3 * width), BF),
+            pltpu.VMEM((PIECE, ff), BF),
+            pltpu.VMEM((length, d), BF),
+            pltpu.VMEM((length, d), BF),
+            pltpu.VMEM((2, n - 1, size, d), BF),
+            pltpu.VMEM((2, 4, half, PIECE), BF),
+            pltpu.VMEM((SIB_SLOTS, 4, half, PIECE), BF),
+            pltpu.VMEM((OWN_SLOTS, 3, half, PIECE), BF),
+            pltpu.VMEM((OWN_SLOTS, half, PIECE), F32),
+            pltpu.VMEM((LINK_SLOTS, 3, half, PIECE), BF),
+            pltpu.VMEM((3, length, 128), F32),
+            pltpu.VMEM((2, 32, d), F32),
+            pltpu.VMEM((8, 8, PIECE), F32),
+            pltpu.VMEM((8, 16, PIECE), F32),
+            pltpu.VMEM((n, 16, PIECE), F32),
+            pltpu.VMEM((8, d), F32),
+            dma((4 * (n - 1),)),
+            dma((4 * (n - 1),)),
+            dma((2,)),
+            dma((SIB_SLOTS,)),
+            dma((OWN_SLOTS, 3)),
+            dma((LINK_SLOTS, 3)),
+            dma((OWN_SLOTS, 2)),
+            dma((6,)),
+            dma((5,)),
+            dma((16 + n - 1,)),
+            dma((16 + n - 1,)),
+            pltpu.SemaphoreType.REGULAR((2,)),
+        ],
+        compiler_params=pltpu.CompilerParams(
+            collective_id=2, has_side_effects=True, vmem_limit_bytes=63 << 20
+        ),
+        cost_estimate=pl.CostEstimate(flops=60_000_000_000, bytes_accessed=100_000_000, transcendentals=0),
+    )(
+        prefix, x, normed, cots, w_qkv, w_up, qkv, joined, branch, attn_grad, up_grad, lse,
+        tables(length), gain[None], jnp.stack([b_out, b_down]),
     )
 
 
@@ -717,112 +1352,24 @@
     w_out, b_out, w_up, b_up, w_down, b_down, prefix, cotangent,
 ):
     n = lax.axis_size("tensor")
-    local_width = w_query.shape[1]
-    hidden_here = w_up.shape[1]
-    heads_here = local_width // HEAD_DIM
-    score_scale = 1.0 / math.sqrt(HEAD_DIM)
-    prefix_len = prefix[0]
-    input_float = layer_input.astype(jnp.float32)
-    row_mean = jnp.mean(input_float, axis=-1, keepdims=True)
-    centred = input_float - row_mean
-    inverse = lax.rsqrt(jnp.mean(centred * centred, axis=-1, keepdims=True) + epsilon)
-    unit_rows = centred * inverse
-    normed_all, grad_all, w_qkv, w_up_all, qkv, joined, part, attn_grad, up_grad_low, lse = forward_call(
+    width = w_query.shape[1]
+    normed, cots, w_qkv, w_up_all, qkv, joined, branch, attn_grad, up_grad, lse = forward_call(
         n, prefix, layer_input, cotangent, w_query, w_key, w_value, w_out, w_up, w_down,
         ln_gain, ln_bias, b_query, b_key, b_value, b_up,
     )
-    length = normed_all.shape[0]
-    positions = jnp.arange(length)
-    block_rows = min(512, length)
-    block_count = length // block_rows
-    query, key, value = (
-        qkv[:, i * local_width : (i + 1) * local_width].reshape(length, heads_here, HEAD_DIM)
-        for i in range(3)
-    )
-    log_totals = lse[:, :heads_here].T.reshape(heads_here, block_count, block_rows).transpose(1, 0, 2)
-
-    def scores_for(query_rows, offset):
-        raw = jnp.einsum("qhd,khd->hqk", query_rows, key, preferred_element_type=jnp.float32)
-        query_pos = offset + jnp.arange(block_rows)
-        seen = (positions[None, :] <= query_pos[:, None]) | (positions[None, :] < prefix_len)
-        return jnp.where(seen[None], raw, masked_score)
-
-    indices = jnp.arange(block_count)
-    branch = lax.psum_scatter(part.astype(F32), "tensor", scatter_dimension=0, tiled=True)
-    layer_out = (input_float + branch + b_out + b_down).astype(jnp.bfloat16)
-    attn_grad_low = attn_grad.reshape(length, heads_here, HEAD_DIM)
-
-    def back_block(carry, item):
-        key_grad, value_grad = carry
-        index, lse_rows = item
-        offset = index * block_rows
-        query_rows = lax.dynamic_slice_in_dim(query, offset, block_rows, 0)
-        grad_rows = lax.dynamic_slice_in_dim(attn_grad_low, offset, block_rows, 0)
-        scores = scores_for(query_rows, offset)
-        probs = jnp.exp(scores - lse_rows[..., None])
-        value_grad = value_grad + jnp.einsum(
-            "hqk,qhd->khd", probs.astype(jnp.bfloat16), grad_rows, preferred_element_type=jnp.float32
-        )
-        prob_grad = jnp.einsum("qhd,khd->hqk", grad_rows, value, preferred_element_type=jnp.float32)
-        delta = jnp.sum(probs * prob_grad, axis=-1, keepdims=True)
-        score_grad = (probs * (prob_grad - delta)).astype(jnp.bfloat16)
-        query_grad = (
-            jnp.einsum("hqk,khd->qhd", score_grad, key, preferred_element_type=jnp.float32) * score_scale
-        )
-        key_grad = key_grad + jnp.einsum(
-            "hqk,qhd->khd", score_grad, query_rows, preferred_element_type=jnp.float32
-        )
-        return ((key_grad, value_grad), query_grad)
-
-    state_zeros = jnp.zeros((length, heads_here, HEAD_DIM), jnp.float32)
-    (key_grad, value_grad), query_blocks = lax.scan(
-        back_block, (state_zeros, state_zeros), (indices, log_totals)
-    )
-    query_grad = query_blocks.reshape(length, heads_here, HEAD_DIM)
-    q_grad_low = rotate(query_grad, positions, -1.0).reshape(length, local_width).astype(jnp.bfloat16)
-    k_grad_low = rotate(key_grad, positions, -1.0).reshape(length, local_width).astype(jnp.bfloat16)
-    v_grad_low = value_grad.reshape(length, local_width).astype(jnp.bfloat16)
-    up_joined = jnp.concatenate([q_grad_low, k_grad_low, v_grad_low, up_grad_low], axis=1)
-    joined_rows = lax.psum_scatter(
-        jnp.concatenate(
-            [rows_transposed(grad_all, joined), rows_transposed(normed_all, up_joined)], axis=1
-        ),
-        "dp",
-        scatter_dimension=0,
-        tiled=True,
-    )
-    down_rows = joined_rows[:, : local_width + hidden_here]
-    up_rows = joined_rows[:, local_width + hidden_here :]
-    d_w_out = down_rows[:, :local_width].T
-    d_w_down = down_rows[:, local_width:].T
-    d_w_query = up_rows[:, :local_width]
-    d_w_key = up_rows[:, local_width : 2 * local_width]
-    d_w_value = up_rows[:, 2 * local_width : 3 * local_width]
-    d_w_up = up_rows[:, 3 * local_width :]
-    part = times_transposed(up_joined[:, : 3 * local_width], w_qkv) + times_transposed(up_grad_low, w_up_all)
-    own_grad = lax.psum_scatter(part, "tensor", scatter_dimension=0, tiled=True)
-    scaled_grad = own_grad * ln_gain
-    norm_part = inverse * (
-        scaled_grad
-        - jnp.mean(scaled_grad, axis=-1, keepdims=True)
-        - unit_rows * jnp.mean(scaled_grad * unit_rows, axis=-1, keepdims=True)
-    )
-    cot_float = cotangent.astype(jnp.float32)
-    d_input = cot_float + norm_part
-    d_ln_gain, d_ln_bias, d_b_out = lax.psum(
-        (
-            jnp.sum(own_grad * unit_rows, axis=0),
-            jnp.sum(own_grad, axis=0),
-            jnp.sum(cot_float, axis=0),
-        ),
-        ("dp", "tensor"),
-    )
-    sums = lax.psum(jnp.sum(up_joined.astype(jnp.float32), axis=0), "dp")
-    d_b_query, d_b_key, d_b_value = (sums[i * local_width : (i + 1) * local_width] for i in range(3))
-    d_b_up = sums[3 * local_width :]
+    layer_out, d_input, d_in, d_dn, d_bias, d_all = backward_call(
+        n, prefix, layer_input, normed, cots, w_qkv, w_up_all, qkv, joined, branch, attn_grad,
+        up_grad, lse, ln_gain, b_out, b_down,
+    )
+    flat, bias = d_all.reshape(-1), d_bias.reshape(-1)
+    d = layer_input.shape[1]
+    d_ln_gain, d_ln_bias, d_b_out = (flat[i * d : (i + 1) * d] for i in range(3))
+    d_w_query, d_w_key, d_w_value = (d_in[:, i * width : (i + 1) * width] for i in range(3))
+    d_b_query, d_b_key, d_b_value = (bias[i * width : (i + 1) * width] for i in range(3))
     return (
         layer_out, d_input, d_ln_gain, d_ln_bias, d_w_query, d_b_query, d_w_key, d_b_key,
-        d_w_value, d_b_value, d_w_out, d_b_out, d_w_up, d_b_up, d_w_down, d_b_out,
+        d_w_value, d_b_value, d_dn[:width], d_b_out, d_in[:, 3 * width :],
+        bias[3 * width : 3 * width + w_up.shape[1]], d_dn[width:], d_b_out,
     )
 
 

time: 983 us -> 392 us (0.40)
  waiting for transfers between devices: 415 us -> 0 us
  Pallas kernels: 187 us -> 372 us
  matrix products: 125 us -> 0 us
  other arithmetic: 83 us -> 2.06 us
  local copies, waits for them, and re-layouts: 83.9 us -> 15.2 us
  blocking collectives: 65.3 us -> 0 us
  between operations: 15 us -> 1.53 us
    reduce_scatter x3 -> x0, waiting for transfers between devices: 415 us -> none  [the longest x1 244 us: on_device(): lax.psum_scatter(jnp.concatenate([rows_transposed(grad_all, joined), rows...]
    pallas_call x0 -> x1, Pallas kernels: none -> 186 us  [backward_call(): pl.pallas_call(functools.partial(backward_scatter, n), out_shape=(shape((...]
    dot_general x14 -> x0, matrix products: 125 us -> none  [the longest x2 42.2 us: rows_transposed(): lax.dot_general(left, right, (((0,), (0,)), ((), ())), preferred_element_...]
    psum x2 -> x0, blocking collectives: 65.3 us -> none  [the longest x1 41.2 us: on_device(): lax.psum((jnp.sum(own_grad * unit_rows, axis=0), jnp.sum(own_grad, axis=0...]
    dynamic_update_slice x4 -> x0, local copies, waits for them, and re-layouts: 43.6 us -> none  [on_device(): lax.scan(back_block, (state_zeros, state_zeros), (indices, log_totals))]
    concatenate x2 -> x0, other arithmetic: 34.3 us -> none  [the longest x1 34.1 us: on_device(): jnp.concatenate([rows_transposed(grad_all, joined), rows_transposed(norme...]
    convert_element_type x5 -> x0, other arithmetic: 30.2 us -> none  [the longest x2 21 us: back_block(): score_grad = (probs * (prob_grad - delta)).astype(jnp.bfloat16)]
    reduce_sum x5 -> x0, other arithmetic: 12.1 us -> none  [the longest x1 5.05 us: on_device(): jnp.sum(cot_float, axis=0)]
  transfers between devices with their start and end apart: 3 -> 0, of which waited for: 3 -> 0; matrix products, arithmetic and copies ran while one was open for 10% -> 0% of each run, Pallas kernels for 0% -> 0%
where the time goes in v2:
time: 392 us; the launch traced here: 391 us
  Pallas kernels  372 us (95%)
  local copies, waits for them, and re-layouts  15.2 us (4%)
    pallas_call x1, Pallas kernels, backward_call(): pl.pallas_call(functools.partial(backward_scatter, n), out_shape=(shape((...  186 us
    pallas_call x1, Pallas kernels, forward_call(): pl.pallas_call(functools.partial(gather_forward, n), out_shape=(shape((le...  186 us

profile of v2, /device:TPU:0, one launch (start us, length us, event | category | flops | bytes accessed | tf_op | source)
XLA Modules:
  0.0 391.0 jit_solution(12183431824803180390)
XLA Ops:
  1.3 0.7 pad_maximum_fusion.1
  2.0 0.6 broadcast_in_dim.15.bqkv
  2.6 1.3 pad_maximum_fusion.b_sum
  4.0 185.8 %shard_map.306 = (bf16[1024,2048]{1,0:T(8,128)(2,1)}, bf16[1024,2048]{1,0:T(8,128)(2,1)}, bf16[2048,1536]{1,0:T(8,128)(2,1)}, bf16[2048,2048]{1,0:T(8,128)(2,1)}...) custom-call(s32[1]{0:T(128)S(6)} %copy.42.prefix, ...), custom_call_target="tpu_custom_call" | custom-call | flops 49999998976 | bytes 100000000 | tf_op jit(solution)/shard_map/pallas_call | solution.py:433
  189.8 186.4 %shard_map.307 = (bf16[256,2048]{1,0:T(8,128)(2,1)}, f32[256,2048]{1,0:T(8,128)}, f32[256,3584]{1,0:T(8,128)}, f32[2560,256]{1,0:T(8,128)}, f32[8,512]{1,0:T(8,128)}, /*index=5*/f32[16,512]{1,0:T(8,128)}) custom-call(s32[1]{0:T(128)S(6)} %copy.42.prefix, bf16[256,2048]{1,0:T(8,128)(2,1)} %x.3, bf16[1024,2048]{1,0:T(8,128)(2,1)} %get-tuple-element.32.normed, ...), custom_call_target="tpu_custom_call" | custom-call | flops 60000002048 | bytes 100000000 | tf_op jit(solution)/shard_map/pallas_call | solution.py:1051
  376.2 0.0 copy-start
  376.2 1.5 fusion.1
  377.7 0.8 slice_bitcast_fusion.1
  378.5 0.0 copy-start.3
  378.5 0.6 copy.36
  379.1 0.6 copy.35
  379.7 0.6 copy.38
  380.3 1.9 slice.73
  382.2 3.0 slice.79
  385.2 0.0 copy-done
  385.2 0.0 copy-start.2
  385.2 1.2 fusion
  386.4 0.0 copy-start.1
  386.4 1.5 slice.76
  387.9 0.0 copy-done.3
  387.9 0.6 copy.43
  388.5 0.0 copy-done.2
  388.5 1.0 copy.44
  389.5 0.0 copy-done.1
  389.5 1.3 copy.45
  (1 shorter events, 0.0 us)
Async XLA Ops:
  376.2 9.1 %copy-start = (f32[256,3584]{1,0:T(8,128)S(1)}, f32[256,3584]{1,0:T(8,128)}, u32[]{:S(2)}) copy-start(f32[256,3584]{1,0:T(8,128)} %get-tuple-element.45) | copy-start | bytes 11010052
  378.5 9.4 %copy-start.3 = (f32[1,4,4,128]{3,1,2,0:T(4,128)}, f32[1,4,4,128]{3,1,2,0:T(4,128)S(1)}, u32[]{:S(2)}) copy-start(f32[1,4,4,128]{3,1,2,0:T(4,128)S(1)} %copy.37) | copy-start | bytes 24580
  385.2 3.3 copy-start.2
  386.4 3.1 copy-start.1
